TPU v7x, 128 devices: a whole 4x4x4 slice. The times are simulated.
128 devices in a mesh: row: 16 (over z, x_lo, core), col: 8 (over y, x_hi).
Axes of the slice: x: 4 (x_hi: 2, x_lo: 2; x = x_hi * 2 + x_lo), y: 4, z: 4, core: 2. Of those that a mesh axis runs over, the one named last changes fastest.
Arguments:
- voxels: bfloat16 [16, 16, 16384], P('row', 'col'), may hold values from -6 to 6
- norm_gain: float32 [64], replicated, may hold values from 0.25 to 1.75
- in_weight: bfloat16 [64, 256], replicated, may hold values from -0.75 to 0.75
- conv_weight: float32 [6, 4, 128], replicated, may hold values from -3 to 3
- conv_bias: float32 [6, 128], replicated, may hold values from -3 to 3
- x_weight: bfloat16 [6, 128, 36], replicated, may hold values from -0.5 to 0.5
- dt_weight: float32 [6, 4, 128], replicated, may hold values from -3 to 3
- dt_bias: float32 [6, 128], replicated, may hold values from -6 to -1
- a_rate: float32 [6, 128, 16], replicated, may hold values from 0.1 to 4
- skip_gain: float32 [6, 128], replicated, may hold values from 0.5 to 1.5
- out_weight: bfloat16 [128, 64], replicated, may hold values from -0.5 to 0.5
Outputs:
- mixed: bfloat16 [16, 16, 16384], P('row', 'col')
All inputs are finite; a program needn't handle non-finite values.
Results may differ from a plain program's by a relative error of at most 0.013.
Values may be sent and summed in bfloat16 or wider, within the bound.
No kernel may reach another device: no remote copies, remote signals or barrier semaphores. Data moves between devices by JAX's collectives and lax.ppermute only.
A program may use at most 64 MiB of HBM per device.

v0:
```python
import math

import jax
import jax.numpy as jnp
from jax import lax
from jax.sharding import PartitionSpec as P


def activation(line_rows, index, conv_weight, conv_bias):
    kernel = conv_weight.shape[1]
    length = line_rows.shape[1]
    values = line_rows.astype(jnp.float32)
    padded = jnp.pad(values, ((0, 0), (kernel - 1, 0), (0, 0)))
    preact = conv_bias[index]
    for offset in range(kernel):
        preact = preact + conv_weight[index, offset] * padded[:, offset : offset + length]
    return jax.nn.silu(preact).astype(jnp.bfloat16)


def run_direction(
    line_rows,
    index,
    reverse,
    conv_weight,
    conv_bias,
    x_weight,
    dt_weight,
    dt_bias,
    a_rate,
    skip_gain,
):
    ordered = line_rows[:, ::-1] if reverse else line_rows
    activated = activation(ordered, index, conv_weight, conv_bias)
    line_count, length, inner_width = activated.shape
    state_n = a_rate.shape[2]
    rank = dt_weight.shape[1]
    projected = jnp.dot(
        activated.reshape(-1, inner_width), x_weight[index], preferred_element_type=jnp.float32
    )
    projected = projected.reshape(line_count, length, -1)
    low_rank = projected[..., :rank]
    b_select = projected[..., rank : rank + state_n]
    c_select = projected[..., rank + state_n :]
    step_size = jax.nn.softplus(
        jnp.einsum("mlr,re->mle", low_rank, dt_weight[index], precision=lax.Precision.HIGHEST)
        + dt_bias[index]
    )
    decay_rate = a_rate[index]
    act_float = activated.astype(jnp.float32)
    block_len = math.gcd(length, 16)
    nblocks = length // block_len

    def regroup(array):
        return jnp.swapaxes(array.reshape(line_count, nblocks, block_len, array.shape[-1]), 0, 1)

    def advance(carried, inputs):
        step_block, act_block, b_block, c_block = inputs
        outputs = []
        for position in range(block_len):
            step_now = step_block[:, position]
            decays = jnp.exp(-step_now[:, :, None] * decay_rate)
            carried = (
                decays * carried
                + (step_now * act_block[:, position])[:, :, None] * b_block[:, position, None, :]
            )
            outputs.append(jnp.sum(carried * c_block[:, position, None, :], axis=2))
        return (carried, jnp.stack(outputs, axis=1))

    start = jnp.zeros((line_count, inner_width, state_n), jnp.float32)
    _, results = lax.scan(
        advance,
        start,
        (regroup(step_size), regroup(act_float), regroup(b_select), regroup(c_select)),
    )
    results = (
        jnp.swapaxes(results, 0, 1).reshape(line_count, length, inner_width)
        + skip_gain[index] * act_float
    )
    return results[:, ::-1] if reverse else results


def both_ways(line_rows, index, params):
    return run_direction(line_rows, index, False, *params) + run_direction(
        line_rows, index + 1, True, *params
    )


def project_inner(normed_rows, in_weight, inner_width):
    return jnp.dot(
        normed_rows, in_weight[:, :inner_width], preferred_element_type=jnp.float32
    ).astype(jnp.bfloat16)


def far_term(sum_rows, silu_gate, out_weight):
    far_hidden = (sum_rows.astype(jnp.float32) * silu_gate).astype(jnp.bfloat16)
    return jnp.dot(far_hidden, out_weight, preferred_element_type=jnp.float32).astype(jnp.bfloat16)


def local(
    voxels,
    norm_gain,
    in_weight,
    conv_weight,
    conv_bias,
    x_weight,
    dt_weight,
    dt_bias,
    a_rate,
    skip_gain,
    out_weight,
):
    params = (conv_weight, conv_bias, x_weight, dt_weight, dt_bias, a_rate, skip_gain)
    width = norm_gain.shape[0]
    inner_width = out_weight.shape[0]
    depth_loc, height_loc, merged = voxels.shape
    z_cells = merged // width
    values = voxels.reshape(depth_loc, height_loc, z_cells, width).astype(jnp.float32)
    normed = (
        values * lax.rsqrt(jnp.mean(values * values, axis=-1, keepdims=True) + 1e-05) * norm_gain
    ).astype(jnp.bfloat16)
    flat_rows = normed.reshape(-1, width)
    inner_z = project_inner(flat_rows, in_weight, inner_width).reshape(
        depth_loc, height_loc, z_cells, inner_width
    )
    gate = jnp.dot(flat_rows, in_weight[:, inner_width:], preferred_element_type=jnp.float32)
    silu_gate = jax.nn.silu(gate)
    along_z = both_ways(inner_z.reshape(depth_loc * height_loc, z_cells, inner_width), 0, params)
    inner_y = lax.all_to_all(inner_z, "col", split_axis=2, concat_axis=1, tiled=True)
    y_full = inner_y.shape[1]
    z_part = inner_y.shape[2]
    along_y = both_ways(
        inner_y.transpose(0, 2, 1, 3).reshape(depth_loc * z_part, y_full, inner_width), 2, params
    )
    sum_y = (
        along_y.reshape(depth_loc, z_part, y_full, inner_width)
        .transpose(0, 2, 1, 3)
        .astype(jnp.bfloat16)
    )
    inner_x, sum_y_x = (
        lax.all_to_all(inner_y, "row", split_axis=1, concat_axis=0, tiled=True),
        lax.all_to_all(sum_y, "row", split_axis=1, concat_axis=0, tiled=True),
    )
    x_full, y_part = (inner_x.shape[0], inner_x.shape[1])
    along_x = both_ways(
        inner_x.transpose(1, 2, 0, 3).reshape(y_part * z_part, x_full, inner_width), 4, params
    )
    along_x = along_x.reshape(y_part, z_part, x_full, inner_width).transpose(2, 0, 1, 3)
    sum_xy = (sum_y_x.astype(jnp.float32) + along_x).astype(jnp.bfloat16)
    returned = lax.all_to_all(
        lax.all_to_all(sum_xy, "row", split_axis=0, concat_axis=1, tiled=True),
        "col",
        split_axis=1,
        concat_axis=2,
        tiled=True,
    )
    far_part = far_term(returned.reshape(-1, inner_width), silu_gate, out_weight)
    near_hidden = (along_z.reshape(-1, inner_width) * silu_gate).astype(jnp.bfloat16)
    mixed = (
        jnp.dot(near_hidden, out_weight, preferred_element_type=jnp.float32)
        + far_part.astype(jnp.float32)
    ).astype(jnp.bfloat16)
    return mixed.reshape(depth_loc, height_loc, merged)


def solution(mesh):
    in_specs = (P("row", "col", None), P(), P(), P(), P(), P(), P(), P(), P(), P(), P())
    out_specs = P("row", "col", None)
    return jax.shard_map(local, mesh=mesh, in_specs=in_specs, out_specs=out_specs, check_vma=False)
```

profile of v0, /device:TPU:1, one launch (start us, length us, event | category | flops | bytes accessed | tf_op | source)
XLA Modules:
  0.0 133.5 jit_solution(2550158983768217386)
XLA Ops:
  0.0 1.0 convert_multiply_fusion
  2.4 0.8 copy.89
  3.2 7.6 %all-to-all-start = ((bf16[1,2,256,128]{3,1,0,2:T(2,128)(2,1)}), bf16[1,2,256,128]{3,1,0,2:T(2,128)(2,1)S(1)}, u32[]{:S(2)}, u32[]{:S(2)}) async-start(bf16[1,2,256,128]{3,1,0,2:T(2,128)(2,1)} %copy.89), calls=%async_computation | async-start | bytes 262144 | tf_op jit(solution)/shard_map/all_to_all | solution.py:128
  17.2 14.4 %while.7 = (s32[]{:T(128)}, f32[2,128,16]{1,2,0:T(8,128)S(1)}, f32[16,2,16,128]{3,2,0,1:T(8,128)S(1)}, f32[16,2,16,128]{3,1,2,0:T(2,128)S(1)}, f32[1,128,16]{1,2...) while((s32[]{:T(128)}, f32[2,128,16]{1,2,0:T(8,128)S(1)}, ...), condition=%wide.region_36.37_spmd.clone, body=%wide.region_19.36_spmd.clone.sunk | while | flops 602115 | bytes 493180 | solution.py:70
  33.5 14.4 %while.6 = (s32[]{:T(128)}, f32[2,128,16]{1,2,0:T(8,128)S(1)}, f32[16,2,16,128]{3,2,0,1:T(8,128)S(1)}, f32[16,2,16,128]{3,1,2,0:T(2,128)S(1)}, f32[1,128,16]{1,2...) while((s32[]{:T(128)}, f32[2,128,16]{1,2,0:T(8,128)S(1)}, ...), condition=%wide.region_18.19_spmd.clone, body=%wide.region_1.18_spmd.clone.sunk | while | flops 602115 | bytes 493180 | solution.py:70
  50.3 0.7 fusion.124
  51.1 1.1 fusion.125
  52.4 1.1 compare_select_fusion.2
  54.1 0.7 fusion.126
  55.5 1.5 %multiply_reduce_fusion.76 = (f32[32,128]{1,0:T(8,128)}, f32[32,128]{1,0:T(8,128)}, f32[32,128]{1,0:T(8,128)}, f32[32,128]{1,0:T(8,128)}) fusion(f32[32,16]{1,0:T(8,128)S(1)} %bitcast.1459, f32[32,16]{1,0:T(8,128)S(1)} %bitcast.1442, f32[32,128]{1,0:T(8,128)S(1)} %bitcast.1368, f32[32,128]{1,0:T(8,128)S(1)} %bitcast.1399, ...), kind=kLoop, calls=%fused_computation.400 | loop fusion | flops 1556480 | bytes 221184 | tf_op jit(solution)/shard_map/while/body/eval_jaxpr/reduce_sum | solution.py:66
  57.0 0.9 multiply_add_fusion.64
  62.2 6.4 %all-to-all-start.2 = ((bf16[1,16,32,128]{3,2,0,1:T(8,128)(2,1)}), bf16[1,16,32,128]{3,2,0,1:T(8,128)(2,1)S(1)}, u32[]{:S(2)}, u32[]{:S(2)}) async-start(bf16[1,16,32,128]{3,2,0,1:T(8,128)(2,1)} %copy.95), calls=%async_computation.2 | async-start | bytes 262144 | tf_op jit(solution)/shard_map/all_to_all | solution.py:140
  69.4 0.7 multiply_reduce_fusion.92
  70.8 0.9 multiply_add_fusion.79
  75.2 5.7 %all-to-all-start.1 = ((bf16[1,16,32,128]{3,2,0,1:T(8,128)(2,1)}), bf16[1,16,32,128]{3,2,0,1:T(8,128)(2,1)S(1)}, u32[]{:S(2)}, u32[]{:S(2)}) async-start(bf16[1,16,32,128]{3,2,0,1:T(8,128)(2,1)} %copy.93), calls=%async_computation.1 | async-start | bytes 262144 | tf_op jit(solution)/shard_map/all_to_all | solution.py:141
  82.7 1.1 compare_select_fusion.1
  84.3 0.7 fusion.128
  85.0 0.8 slice_negate_fusion.25
  85.8 1.1 fusion.129
  88.7 1.1 compare_select_fusion
  90.3 0.7 fusion.130
  91.7 1.3 %multiply_reduce_fusion.44 = (f32[32,128]{1,0:T(8,128)S(1)}, f32[32,128]{1,0:T(8,128)S(1)}, f32[32,128]{1,0:T(8,128)S(1)}, f32[32,128]{1,0:T(8,128)}) fusion(f32[32,16]{1,0:T(8,128)S(1)} %bitcast.1463, f32[32,16]{1,0:T(8,128)S(1)} %bitcast.1451, f32[32,128]{1,0:T(8,128)S(1)} %bitcast.1380, f32[32,128]{1,0:T(8,128)S(1)} %bitcast.1407, ...), kind=kLoop, calls=%fused_computation.334 | loop fusion | flops 1556480 | bytes 221184 | tf_op jit(solution)/shard_map/while/body/eval_jaxpr/reduce_sum | solution.py:66
  93.1 0.9 multiply_add_fusion.33
  95.7 0.7 copy-done.11
  98.4 1.0 multiply_reduce_fusion.60
  100.1 0.9 multiply_add_fusion.48
  104.5 5.7 %all-to-all-start.3 = ((bf16[16,1,32,128]{3,2,1,0:T(8,128)(2,1)}), bf16[16,1,32,128]{3,2,1,0:T(8,128)(2,1)}, u32[]{:S(2)}, u32[]{:S(2)}) async-start(bf16[16,1,32,128]{3,2,1,0:T(8,128)(2,1)} %copy.99), calls=%async_computation.3 | async-start | bytes 262144 | tf_op jit(solution)/shard_map/all_to_all | solution.py:150
  111.3 5.2 %all-to-all-done.3 = bf16[16,1,32,128]{3,2,1,0:T(8,128)(2,1)} async-done(((bf16[16,1,32,128]{3,2,1,0:T(8,128)(2,1)}), bf16[16,1,32,128]{3,2,1,0:T(8,128)(2,1)}, u32[]{:S(2)}, u32[]{:S(2)}) %all-to-all-start.3) | async-done | bytes 131104 | tf_op jit(solution)/shard_map/all_to_all | solution.py:150
  116.5 7.5 %all-to-all-start.4 = ((bf16[1,16,32,128]{3,2,0,1:T(8,128)(2,1)}), bf16[1,16,32,128]{3,2,0,1:T(8,128)(2,1)S(1)}, u32[]{:S(2)}, u32[]{:S(2)}) async-start(bf16[1,16,32,128]{3,2,0,1:T(8,128)(2,1)} %bitcast.432), calls=%async_computation.4 | async-start | bytes 262144 | tf_op jit(solution)/shard_map/all_to_all | solution.py:149
  124.9 6.2 %all-to-all-done.4 = bf16[1,16,32,128]{3,2,0,1:T(8,128)(2,1)S(1)} async-done(((bf16[1,16,32,128]{3,2,0,1:T(8,128)(2,1)}), bf16[1,16,32,128]{3,2,0,1:T(8,128)(2,1)S(1)}, u32[]{:S(2)}, u32[]{:S(2)}) %all-to-all-start.4) | async-done | bytes 131104 | tf_op jit(solution)/shard_map/all_to_all | solution.py:149
  131.1 0.7 copy-done.32
  132.7 0.8 reshape.1952
  (699 shorter events, 63.3 us)
Async XLA Ops:
  0.0 132.2 %copy-start = (bf16[128,64]{0,1:T(8,128)(2,1)S(1)}, bf16[128,64]{0,1:T(8,128)(2,1)}, u32[]{:S(2)}) copy-start(bf16[128,64]{0,1:T(8,128)(2,1)} %param.25) | copy-start | bytes 49156
  0.0 1.0 copy-start.1
  3.2 7.6 %copy-start.30 = (f32[6,4,128]{2,1,0:T(4,128)S(1)}, f32[6,4,128]{2,1,0:T(4,128)}, u32[]{:S(2)}) copy-start(f32[6,4,128]{2,1,0:T(4,128)} %param.18) | copy-start | bytes 36868
  3.2 45.4 %all-to-all-start = ((bf16[1,2,256,128]{3,1,0,2:T(2,128)(2,1)}), bf16[1,2,256,128]{3,1,0,2:T(2,128)(2,1)S(1)}, u32[]{:S(2)}, u32[]{:S(2)}) async-start(bf16[1,2,256,128]{3,1,0,2:T(2,128)(2,1)} %copy.89), calls=%async_computation | async-start | bytes 262144 | tf_op jit(solution)/shard_map/all_to_all | solution.py:128
  11.4 2.7 %copy-start.43 = (f32[128]{0:T(128)}, f32[128]{0:T(128)S(1)}, u32[]{:S(2)}) copy-start(f32[128]{0:T(128)S(1)} %get-tuple-element.818) | copy-start | bytes 1540
  11.4 2.7 %copy-start.45 = (f32[128]{0:T(128)}, f32[128]{0:T(128)S(1)}, u32[]{:S(2)}) copy-start(f32[128]{0:T(128)S(1)} %get-tuple-element.819) | copy-start | bytes 1540
  11.4 2.7 %copy-start.47 = (f32[128]{0:T(128)}, f32[128]{0:T(128)S(1)}, u32[]{:S(2)}) copy-start(f32[128]{0:T(128)S(1)} %get-tuple-element.820) | copy-start | bytes 1540
  11.4 2.7 %copy-start.49 = (f32[128]{0:T(128)}, f32[128]{0:T(128)S(1)}, u32[]{:S(2)}) copy-start(f32[128]{0:T(128)S(1)} %get-tuple-element.821) | copy-start | bytes 1540
  11.4 20.2 %copy-start.33 = (f32[128]{0:T(128)}, f32[128]{0:T(128)S(1)}, u32[]{:S(2)}) copy-start(f32[128]{0:T(128)S(1)} %get-tuple-element.803) | copy-start | bytes 1540
  12.0 19.6 %copy-start.35 = (f32[128]{0:T(128)}, f32[128]{0:T(128)S(1)}, u32[]{:S(2)}) copy-start(f32[128]{0:T(128)S(1)} %get-tuple-element.822) | copy-start | bytes 1540
  12.0 19.6 %copy-start.37 = (f32[128]{0:T(128)}, f32[128]{0:T(128)S(1)}, u32[]{:S(2)}) copy-start(f32[128]{0:T(128)S(1)} %get-tuple-element.823) | copy-start | bytes 1540
  12.0 19.6 %copy-start.39 = (f32[128]{0:T(128)}, f32[128]{0:T(128)S(1)}, u32[]{:S(2)}) copy-start(f32[128]{0:T(128)S(1)} %get-tuple-element.824) | copy-start | bytes 1540
  12.2 1.9 %copy-start.3 = (f32[6,128,16]{1,2,0:T(8,128)S(1)}, f32[6,128,16]{1,2,0:T(8,128)}, u32[]{:S(2)}) copy-start(f32[6,128,16]{1,2,0:T(8,128)} %param.23) | copy-start | bytes 147460
  12.3 1.2 copy-start.54
  13.5 18.2 %copy-start.41 = (f32[128]{0:T(128)}, f32[128]{0:T(128)S(1)}, u32[]{:S(2)}) copy-start(f32[128]{0:T(128)S(1)} %get-tuple-element.833) | copy-start | bytes 1540
  33.5 14.4 %copy-start.55 = (f32[6,128]{1,0:T(8,128)S(1)}, f32[6,128]{1,0:T(8,128)}, u32[]{:S(2)}) copy-start(f32[6,128]{1,0:T(8,128)} %param.24) | copy-start | bytes 9220
  62.2 6.5 %copy-start.20 = (f32[32,1,16]{2,1,0:T(1,128)S(1)}, f32[32,1,16]{2,1,0:T(1,128)}, u32[]{:S(2)}) copy-start(f32[32,1,16]{2,1,0:T(1,128)} %get-tuple-element.631) | copy-start | bytes 6148
  62.2 6.5 %copy-start.21 = (f32[32,1,16]{2,1,0:T(1,128)S(1)}, f32[32,1,16]{2,1,0:T(1,128)}, u32[]{:S(2)}) copy-start(f32[32,1,16]{2,1,0:T(1,128)} %get-tuple-element.633) | copy-start | bytes 6148
  62.2 6.5 %copy-start.26 = (f32[32,1,16]{2,1,0:T(1,128)S(1)}, f32[32,1,16]{2,1,0:T(1,128)}, u32[]{:S(2)}) copy-start(f32[32,1,16]{2,1,0:T(1,128)} %get-tuple-element.626) | copy-start | bytes 6148
  62.2 6.5 %copy-start.27 = (f32[32,1,16]{2,1,0:T(1,128)S(1)}, f32[32,1,16]{2,1,0:T(1,128)}, u32[]{:S(2)}) copy-start(f32[32,1,16]{2,1,0:T(1,128)} %get-tuple-element.628) | copy-start | bytes 6148
  62.2 6.5 %copy-start.28 = (f32[32,1,16]{2,1,0:T(1,128)S(1)}, f32[32,1,16]{2,1,0:T(1,128)}, u32[]{:S(2)}) copy-start(f32[32,1,16]{2,1,0:T(1,128)} %get-tuple-element.630) | copy-start | bytes 6148
  62.2 6.5 %copy-start.29 = (f32[32,1,16]{2,1,0:T(1,128)S(1)}, f32[32,1,16]{2,1,0:T(1,128)}, u32[]{:S(2)}) copy-start(f32[32,1,16]{2,1,0:T(1,128)} %get-tuple-element.632) | copy-start | bytes 6148
  62.2 13.0 %all-to-all-start.2 = ((bf16[1,16,32,128]{3,2,0,1:T(8,128)(2,1)}), bf16[1,16,32,128]{3,2,0,1:T(8,128)(2,1)S(1)}, u32[]{:S(2)}, u32[]{:S(2)}) async-start(bf16[1,16,32,128]{3,2,0,1:T(8,128)(2,1)} %copy.95), calls=%async_computation.2 | async-start | bytes 262144 | tf_op jit(solution)/shard_map/all_to_all | solution.py:140
  75.2 27.9 %all-to-all-start.1 = ((bf16[1,16,32,128]{3,2,0,1:T(8,128)(2,1)}), bf16[1,16,32,128]{3,2,0,1:T(8,128)(2,1)S(1)}, u32[]{:S(2)}, u32[]{:S(2)}) async-start(bf16[1,16,32,128]{3,2,0,1:T(8,128)(2,1)} %copy.93), calls=%async_computation.1 | async-start | bytes 262144 | tf_op jit(solution)/shard_map/all_to_all | solution.py:141
  103.8 6.5 %copy-start.50 = (f32[128]{0:T(128)S(1)}, f32[128]{0:T(128)}, u32[]{:S(2)}) copy-start(f32[128]{0:T(128)} %copy-done.49) | copy-start | bytes 1540
  103.8 6.5 %copy-start.52 = (f32[128]{0:T(128)S(1)}, f32[128]{0:T(128)}, u32[]{:S(2)}) copy-start(f32[128]{0:T(128)} %copy-done.51) | copy-start | bytes 1540
  103.8 6.5 %copy-start.57 = (f32[128]{0:T(128)S(1)}, f32[128]{0:T(128)}, u32[]{:S(2)}) copy-start(f32[128]{0:T(128)} %get-tuple-element.830) | copy-start | bytes 1540
  104.5 12.0 %all-to-all-start.3 = ((bf16[16,1,32,128]{3,2,1,0:T(8,128)(2,1)}), bf16[16,1,32,128]{3,2,1,0:T(8,128)(2,1)}, u32[]{:S(2)}, u32[]{:S(2)}) async-start(bf16[16,1,32,128]{3,2,1,0:T(8,128)(2,1)} %copy.99), calls=%async_computation.3 | async-start | bytes 262144 | tf_op jit(solution)/shard_map/all_to_all | solution.py:150
  111.1 12.9 %copy-start.40 = (f32[128]{0:T(128)S(1)}, f32[128]{0:T(128)}, u32[]{:S(2)}) copy-start(f32[128]{0:T(128)} %copy-done.39) | copy-start | bytes 1540
  111.2 12.9 %copy-start.42 = (f32[128]{0:T(128)S(1)}, f32[128]{0:T(128)}, u32[]{:S(2)}) copy-start(f32[128]{0:T(128)} %copy-done.41) | copy-start | bytes 1540
  111.2 12.9 %copy-start.56 = (f32[128]{0:T(128)S(1)}, f32[128]{0:T(128)}, u32[]{:S(2)}) copy-start(f32[128]{0:T(128)} %get-tuple-element.827) | copy-start | bytes 1540
  116.5 14.6 %all-to-all-start.4 = ((bf16[1,16,32,128]{3,2,0,1:T(8,128)(2,1)}), bf16[1,16,32,128]{3,2,0,1:T(8,128)(2,1)S(1)}, u32[]{:S(2)}, u32[]{:S(2)}) async-start(bf16[1,16,32,128]{3,2,0,1:T(8,128)(2,1)} %bitcast.432), calls=%async_computation.4 | async-start | bytes 262144 | tf_op jit(solution)/shard_map/all_to_all | solution.py:149
  (50 other events, 34.7 us)
where the time goes:
time: 136 us; the launch traced here: 133 us
  other arithmetic  43.6 us (32%)
  local copies, waits for them, and re-layouts  34.2 us (25%)
  starting transfers between devices  33 us (24%)
  waiting for transfers between devices  11.4 us (8%)
  matrix products  7.08 us (5%)
  loops' own time  2.86 us (2%)
    reduce_sum x176, other arithmetic, advance(): outputs.append(jnp.sum(carried * c_block[:, position, None, :], axis=2))  32.8 us
    unnamed x155, local copies, waits for them, and re-layouts  13.9 us
    all_to_all x1, starting transfers between devices, local(): lax.all_to_all(inner_z, 'col', split_axis=2, concat_axis=1, tiled=True)  7.61 us
    all_to_all x1, starting transfers between devices, local(): lax.all_to_all(lax.all_to_all(sum_xy, 'row', split_axis=0, concat_axis=1,...  7.52 us
    all_to_all x1, starting transfers between devices, local(): lax.all_to_all(inner_y, 'row', split_axis=1, concat_axis=0, tiled=True)  6.45 us
    all_to_all x1, waiting for transfers between devices, local(): lax.all_to_all(lax.all_to_all(sum_xy, 'row', split_axis=0, concat_axis=1,...  6.17 us
    slice x8, local copies, waits for them, and re-layouts, advance(): outputs.append(jnp.sum(carried * c_block[:, position, None, :], axis=2))  6.14 us
    all_to_all x1, starting transfers between devices, local(): lax.all_to_all(sum_y, 'row', split_axis=1, concat_axis=0, tiled=True)  5.72 us
  transfers between devices with their start and end apart: 5, of which 2 were waited for; matrix products, arithmetic and copies ran while one was open for 41% of the time, Pallas kernels for 0%

commit v1 on v0

v1 whole, which is shorter than its diff:
```python
import functools
import math

import jax
import jax.numpy as jnp
from jax import lax
from jax.experimental import pallas as pl
from jax.experimental.pallas import tpu as pltpu
from jax.sharding import PartitionSpec as P

C = 64
E = 128
N = 16
R = 4
K = 4
Q = 4
EQ = E // Q
STEPS = 16
LINES = 32
A0, CW0, CB0, DW0, DB0, SK0, ROWS = 0, 16, 20, 21, 25, 26, 27
LOG2E = math.log2(math.e)
F32 = jnp.float32
BF16 = jnp.bfloat16
HIGHEST = lax.Precision.HIGHEST
NT = (((1,), (1,)), ((), ()))
VMEM_LIMIT = 48 * 1024 * 1024


def iota(shape, axis):
    return lax.broadcasted_iota(jnp.int32, shape, axis)


def silu(x):
    half = 0.5 * x
    return half * (1.0 + jnp.tanh(half))


def softplus(x):
    tail = jnp.exp2(jnp.abs(x) * (-LOG2E))
    return jnp.maximum(x, 0.0) + jnp.where(tail < 1e-4, tail, jnp.log(1.0 + tail))


def prepare_kernel(in_w, conv_w, conv_b, x_w, dt_w, dt_b, a_rate, skip, out_w, gain, table, lhsq, xp, wo, gain2):
    mask = ((iota((EQ, E), 1) % EQ) == iota((EQ, E), 0)).astype(F32)
    same = (iota((E, E), 0) // EQ == iota((E, E), 1) // EQ).astype(F32)
    eye = (iota((N, N), 0) == iota((N, N), 1)).astype(F32)
    row, column = iota((40, 36), 0), iota((40, 36), 1)
    pick = (column == jnp.where(row < 2 * N, row + R, row - 2 * N)) & (row < 2 * N + R)
    pick = pick.astype(BF16)
    for d in range(6):
        rates = lax.dot_general(eye, a_rate[d], NT, precision=HIGHEST, preferred_element_type=F32)
        rows = jnp.concatenate(
            [
                rates * (-LOG2E),
                conv_w[d],
                conv_b[d : d + 1, :],
                dt_w[d],
                dt_b[d : d + 1, :],
                skip[d : d + 1, :],
            ],
            axis=0,
        )
        spread = (rows[:, None, :] * mask[None]).reshape(ROWS * EQ, E)
        table[d] = jnp.dot(spread, same, precision=HIGHEST, preferred_element_type=F32).reshape(ROWS, EQ, E)
        xp[d] = lax.dot_general(pick, x_w[d], NT, preferred_element_type=F32).astype(BF16)
    turned = in_w[...].astype(F32).T
    for part in range(2):
        blocks = [turned[part * E + q * EQ : part * E + (q + 1) * EQ] for q in range(Q)]
        lhsq[part * EQ : (part + 1) * EQ, :] = jnp.concatenate(blocks, axis=1).astype(BF16)
    wide = jnp.concatenate([out_w[...], out_w[...]], axis=1)
    low = iota((EQ, 2 * C), 1) < C
    zero = jnp.zeros((EQ, 2 * C), BF16)
    for q in range(Q):
        block = wide[q * EQ : (q + 1) * EQ]
        wo[q, 0] = jnp.where(low, block, zero)
        wo[q, 1] = jnp.where(low, zero, block)
    gain2[...] = jnp.concatenate([gain[...], gain[...]], axis=1)


def normalise(values, gain2, plain, rolled):
    low = iota(values.shape, 1) < C
    squares = values * values
    first = jnp.sum(jnp.where(low, squares, 0.0), axis=1, keepdims=True) * (1.0 / C)
    second = jnp.sum(jnp.where(low, 0.0, squares), axis=1, keepdims=True) * (1.0 / C)
    scale = jnp.where(low, lax.rsqrt(first + 1e-05), lax.rsqrt(second + 1e-05))
    normed = (values * scale * gain2).astype(BF16).astype(F32)
    plain[...] = normed
    rolled[...] = pltpu.roll(normed, C, 1)


def project(blocks, lhsq):
    half = jnp.concatenate(blocks, axis=0)
    zero = jnp.zeros_like(half)
    rows = jnp.concatenate(
        [jnp.concatenate([half, zero], axis=1), jnp.concatenate([zero, half], axis=1)], axis=0
    ).astype(BF16)
    both = lax.dot_general(lhsq, rows, NT, preferred_element_type=F32)
    return both[:EQ].astype(BF16).astype(F32), both[EQ:]


def step_inputs(d, index, neighbours, table, xp, quarter, act_s, sel_s, step_s, fresh_s):
    pre = table[index, CB0]
    for k in range(K):
        if neighbours[k] is not None:
            pre = pre + table[index, CW0 + k] * neighbours[k]
    act = silu(pre).astype(BF16).astype(F32)
    spread = jnp.concatenate([jnp.where(quarter == q, act, 0.0) for q in range(Q)], axis=0).astype(BF16)
    sel = jnp.dot(xp[index], spread, preferred_element_type=F32)
    sel = sel + pltpu.roll(sel, 64, 1)
    sel = sel + pltpu.roll(sel, 32, 1)
    raw = table[index, DB0]
    for r in range(R):
        raw = raw + table[index, DW0 + r] * sel[2 * N + r : 2 * N + r + 1, :]
    step = softplus(raw)
    return act, sel, step


def scan_group(index, d, rows, start, table, sel_s, step_s, fresh_s, y_s):
    rates = [table[index, A0 + n, rows, :] for n in range(N)]
    state = start
    for s in range(STEPS):
        t = s if d == 0 else STEPS - 1 - s
        step = step_s[d, t, rows, :]
        fresh = fresh_s[d, t, rows, :]
        total = [None, None]
        following = []
        for n in range(N):
            new = fresh * sel_s[d, t, n : n + 1, :]
            if state is not None:
                new = new + jnp.exp2(step * rates[n]) * state[n]
            following.append(new)
            term = new * sel_s[d, t, N + n : N + n + 1, :]
            total[n % 2] = term if total[n % 2] is None else total[n % 2] + term
        state = following
        y_s[t, rows, :] = y_s[t, rows, :] + (total[0] + total[1])
    return state


def gated_rows(y_s, gate_s, turned_s):
    for t in range(STEPS):
        turned_s[t] = (y_s[t] * gate_s[t]).T


def plane_kernel(values, table, lhsq_ref, xp, wo, gain2, out, plain, rolled, inner_s, gate_s, act_s, sel_s, step_s, fresh_s, y_s, turned_s, far_s):
    normalise(values[...].astype(F32), gain2[...], plain, rolled)
    quarter = iota((EQ, E), 1) // LINES
    low = iota((STEPS, 2 * C), 1) < C
    lhsq = lhsq_ref[...]
    for axis in range(2):
        for t in range(STEPS):
            where = pl.ds(t, STEPS, stride=STEPS) if axis == 0 else pl.ds(t * STEPS, STEPS)
            own, swapped = plain[where, :], rolled[where, :]
            blocks = [
                jnp.where(low, own, 0.0),
                jnp.where(low, swapped, 0.0),
                jnp.where(low, 0.0, swapped),
                jnp.where(low, 0.0, own),
            ]
            inner, gate = project(blocks, lhsq)
            inner_s[t] = inner
            gate_s[t] = silu(gate)
        for d in range(2):
            index = 2 + 2 * axis + d
            for t in range(STEPS):
                near = [t - 3 + k if d == 0 else t + 3 - k for k in range(K)]
                near = [inner_s[p] if 0 <= p < STEPS else None for p in near]
                act, sel, step = step_inputs(d, index, near, table, xp, quarter, act_s, sel_s, step_s, fresh_s)
                sel_s[d, t] = sel
                step_s[d, t] = step
                fresh_s[d, t] = step * act
                direct = table[index, SK0] * act
                y_s[t] = direct if d == 0 else y_s[t] + direct

        def group(g, carry):
            rows = pl.ds(pl.multiple_of(g * 8, 8), 8)
            for d in range(2):
                scan_group(2 + 2 * axis + d, d, rows, None, table, sel_s, step_s, fresh_s, y_s)
            return carry

        lax.fori_loop(0, EQ // 8, group, 0)
        gated_rows(y_s, gate_s, turned_s)
        far = None
        for q in range(Q):
            for half in range(2):
                first = (2 * q + half) * STEPS
                lhs = turned_s[:, first : first + STEPS, :].reshape(STEPS * STEPS, EQ).astype(BF16)
                part = jnp.dot(lhs, wo[q, half], preferred_element_type=F32)
                far = part if far is None else far + part
        if axis == 0:
            for t in range(STEPS):
                far_s[pl.ds(t, STEPS, stride=STEPS), :] = far[t * STEPS : (t + 1) * STEPS]
        else:
            out[...] = (far + far_s[...]).astype(BF16)


def line_kernel(values, table, lhsq_ref, xp, wo, gain2, out, plain, rolled, inner_s, gate_s, act_s, sel_s, step_s, fresh_s, y_s, turned_s, end_s):
    normalise(values[...].astype(F32), gain2[...], plain, rolled)
    lane = iota((EQ, E), 1)
    quarter = lane // LINES
    chunk = lane % STEPS
    low = iota((STEPS, 2 * C), 1) < C
    lhsq = lhsq_ref[...]
    for t in range(STEPS):
        blocks = []
        for half in range(2):
            for y in range(2):
                where = pl.ds(y * 128 + t // 2, STEPS, stride=8)
                rows = plain[where, :] if t % 2 == half else rolled[where, :]
                blocks.append(jnp.where(low, rows, 0.0) if half == 0 else jnp.where(low, 0.0, rows))
        inner, gate = project(blocks, lhsq)
        inner_s[t] = inner
        gate_s[t] = silu(gate)
    for d in range(2):
        edge = (chunk >= 1) if d == 0 else (chunk < STEPS - 1)
        for t in range(STEPS):
            near = []
            for k in range(K):
                p = t - 3 + k if d == 0 else t + 3 - k
                if 0 <= p < STEPS:
                    near.append(inner_s[p])
                else:
                    moved = pltpu.roll(inner_s[p % STEPS], 1 if d == 0 else E - 1, 1)
                    near.append(jnp.where(edge, moved, 0.0))
            act, sel, step = step_inputs(d, d, near, table, xp, quarter, act_s, sel_s, step_s, fresh_s)
            sel_s[d, t] = sel
            step_s[d, t] = step
            fresh_s[d, t] = step * act
            direct = table[d, SK0] * act
            y_s[t] = direct if d == 0 else y_s[t] + direct

    far_off = 1e4

    def group(g, carry):
        rows = pl.ds(pl.multiple_of(g * 8, 8), 8)
        place = iota((8, E), 1) % STEPS
        for d in range(2):
            rates = [table[d, A0 + n, rows, :] for n in range(N)]
            ends = None
            whole = None
            for s in range(STEPS):
                t = s if d == 0 else STEPS - 1 - s
                step = step_s[d, t, rows, :]
                fresh = fresh_s[d, t, rows, :]
                whole = step if whole is None else whole + step
                following = []
                for n in range(N):
                    new = fresh * sel_s[d, t, n : n + 1, :]
                    if ends is not None:
                        new = new + jnp.exp2(step * rates[n]) * ends[n]
                    following.append(new)
                ends = following
            for k in (1, 2, 4, 8):
                by = k if d == 0 else E - k
                inside = (place >= k) if d == 0 else (place < STEPS - k)
                span = jnp.where(inside, whole, far_off)
                ends = [e + jnp.exp2(span * a) * pltpu.roll(e, by, 1) for e, a in zip(ends, rates)]
                whole = whole + jnp.where(inside, pltpu.roll(whole, by, 1), 0.0)
            by = 1 if d == 0 else E - 1
            inside = (place >= 1) if d == 0 else (place < STEPS - 1)
            start = [jnp.where(inside, pltpu.roll(e, by, 1), 0.0) for e in ends]
            scan_group(d, d, rows, start, table, sel_s, step_s, fresh_s, y_s)
        return carry

    lax.fori_loop(0, EQ // 8, group, 0)
    gated_rows(y_s, gate_s, turned_s)
    near = None
    for q in range(Q):
        for half in range(2):
            steps = [turned_s[2 * p + half, q * LINES : (q + 1) * LINES, :] for p in range(8)]
            lhs = jnp.concatenate(steps, axis=0).astype(BF16)
            part = jnp.dot(lhs, wo[q, half], preferred_element_type=F32)
            near = part if near is None else near + part
    for p in range(8):
        for y in range(2):
            first = p * LINES + y * STEPS
            out[pl.ds(2 * p + y, STEPS, stride=16), :] = near[first : first + STEPS]


def vmem(count):
    return [pl.BlockSpec(memory_space=pltpu.VMEM)] * count


def scan_scratch():
    return [
        pltpu.VMEM((256, E), F32),
        pltpu.VMEM((256, E), F32),
        pltpu.VMEM((STEPS, EQ, E), F32),
        pltpu.VMEM((STEPS, EQ, E), F32),
        pltpu.VMEM((2, STEPS, EQ, E), F32),
        pltpu.VMEM((2, STEPS, 40, E), F32),
        pltpu.VMEM((2, STEPS, EQ, E), F32),
        pltpu.VMEM((2, STEPS, EQ, E), F32),
        pltpu.VMEM((STEPS, EQ, E), F32),
        pltpu.VMEM((STEPS, E, EQ), F32),
    ]


PARAMS = pltpu.CompilerParams(vmem_limit_bytes=VMEM_LIMIT)


def prepare(*weights):
    shapes = [
        jax.ShapeDtypeStruct((6, ROWS, EQ, E), F32),
        jax.ShapeDtypeStruct((2 * EQ, Q * C), BF16),
        jax.ShapeDtypeStruct((6, 40, E), BF16),
        jax.ShapeDtypeStruct((Q, 2, EQ, 2 * C), BF16),
        jax.ShapeDtypeStruct((1, 2 * C), F32),
    ]
    return pl.pallas_call(
        prepare_kernel, out_shape=shapes, in_specs=vmem(10), out_specs=vmem(5), compiler_params=PARAMS, name="prepare"
    )(*weights)


def planes(values, ready):
    return pl.pallas_call(
        plane_kernel,
        out_shape=jax.ShapeDtypeStruct((256, 2 * C), BF16),
        in_specs=vmem(6),
        out_specs=vmem(1)[0],
        scratch_shapes=scan_scratch() + [pltpu.VMEM((256, 2 * C), F32)],
        compiler_params=PARAMS,
        name="planes",
    )(values, *ready)


def z_lines(values, ready):
    return pl.pallas_call(
        line_kernel,
        out_shape=jax.ShapeDtypeStruct((256, 2 * C), F32),
        in_specs=vmem(6),
        out_specs=vmem(1)[0],
        scratch_shapes=scan_scratch() + [pltpu.VMEM((8, E), F32)],
        compiler_params=PARAMS,
        name="z_lines",
    )(values, *ready)


def local(voxels, norm_gain, in_weight, conv_weight, conv_bias, x_weight, dt_weight, dt_bias, a_rate, skip_gain, out_weight):
    pairs = voxels.reshape(2, 128, 2 * C)
    sent = pairs.transpose(1, 0, 2)
    arrived = lax.all_to_all(sent, ("row", "col"), split_axis=0, concat_axis=0, tiled=True)
    ready = prepare(
        in_weight, conv_weight, conv_bias, x_weight, dt_weight, dt_bias, a_rate, skip_gain, out_weight, norm_gain.reshape(1, C)
    )
    far = planes(arrived.reshape(256, 2 * C), ready)
    returned = lax.all_to_all(far.reshape(128, 2, 2 * C), ("row", "col"), split_axis=0, concat_axis=0, tiled=True)
    near = z_lines(pairs.reshape(256, 2 * C), ready)
    mixed = (near.reshape(128, 2, 2 * C) + returned.astype(F32)).astype(BF16)
    return mixed.transpose(1, 0, 2).reshape(1, 2, 128 * 2 * C)


def solution(mesh):
    in_specs = (P("row", "col", None),) + (P(),) * 10
    return jax.shard_map(local, mesh=mesh, in_specs=in_specs, out_specs=P("row", "col", None), check_vma=False)
```

time: 136 us -> 51.8 us (0.38); the launches traced: 133 us -> 51.3 us
  other arithmetic: 43.6 us -> 0.7 us
  local copies, waits for them, and re-layouts: 34.2 us -> 7.75 us
  Pallas kernels: 0 us -> 18.9 us
  starting transfers between devices: 33 us -> 21.3 us
  waiting for transfers between devices: 11.4 us -> 2.57 us
  matrix products: 7.08 us -> 0 us
  loops' own time: 2.86 us -> 0 us
    reduce_sum x177 -> x0, other arithmetic: 33 us -> none  [the longest x176 32.8 us: advance(): outputs.append(jnp.sum(carried * c_block[:, position, None, :], axis=2))]
    pallas_call x0 -> x3, Pallas kernels: none -> 18.9 us  [the longest x1 8.18 us: planes(): pl.pallas_call(plane_kernel, out_shape=jax.ShapeDtypeStruct((256, 2 * C),...]
    all_to_all x5 -> x2, starting transfers between devices: 33 us -> 21.3 us  [the longest x1 11.5 us: local(): lax.all_to_all(sent, ('row', 'col'), split_axis=0, concat_axis=0, tiled=T...]
    all_to_all x5 -> x2, waiting for transfers between devices: 11.4 us -> 2.57 us  [the longest x1 2.56 us: local(): lax.all_to_all(far.reshape(128, 2, 2 * C), ('row', 'col'), split_axis=0,...]
    dot_general x16 -> x0, matrix products: 7.08 us -> none  [the longest x6 5.21 us: run_direction(): jnp.einsum('mlr,re->mle', low_rank, dt_weight[index], precision=lax.Preci...]
    unnamed x155 -> x19, local copies, waits for them, and re-layouts: 13.9 us -> 7.69 us
    slice x11 -> x0, local copies, waits for them, and re-layouts: 6.17 us -> none  [the longest x8 6.14 us: advance(): outputs.append(jnp.sum(carried * c_block[:, position, None, :], axis=2))]
    add x8 -> x0, other arithmetic: 4.23 us -> none  [the longest x4 3.77 us: advance(): decays * carried]
  transfers between devices with their start and end apart: 5 -> 2, of which waited for: 2 -> 1; matrix products, arithmetic and copies ran while one was open for 41% -> 6% of each run, Pallas kernels for 0% -> 21%
where the time goes in v1:
time: 51.8 us; the launch traced here: 51.3 us
  starting transfers between devices  21.3 us (41%)
  Pallas kernels  18.9 us (36%)
  local copies, waits for them, and re-layouts  7.75 us (15%)
  waiting for transfers between devices  2.57 us (5%)
  other arithmetic  0.7 us (1%)
    all_to_all x1, starting transfers between devices, local(): lax.all_to_all(sent, ('row', 'col'), split_axis=0, concat_axis=0, tiled=T...  11.5 us
    all_to_all x1, starting transfers between devices, local(): lax.all_to_all(far.reshape(128, 2, 2 * C), ('row', 'col'), split_axis=0,...  9.76 us
    pallas_call x1, Pallas kernels, planes(): pl.pallas_call(plane_kernel, out_shape=jax.ShapeDtypeStruct((256, 2 * C),...  8.18 us
    unnamed x19, local copies, waits for them, and re-layouts  7.69 us
    pallas_call x1, Pallas kernels, z_lines(): pl.pallas_call(line_kernel, out_shape=jax.ShapeDtypeStruct((256, 2 * C),...  7.16 us
    pallas_call x1, Pallas kernels, prepare(): pl.pallas_call(prepare_kernel, out_shape=shapes, in_specs=vmem(10), out_s...  3.55 us
    all_to_all x1, waiting for transfers between devices, local(): lax.all_to_all(far.reshape(128, 2, 2 * C), ('row', 'col'), split_axis=0,...  2.56 us
  transfers between devices with their start and end apart: 2, of which 1 were waited for; matrix products, arithmetic and copies ran while one was open for 6% of the time, Pallas kernels for 21%

profile of v1, /device:TPU:1, one launch (start us, length us, event | category | flops | bytes accessed | tf_op | source)
XLA Modules:
  0.0 51.3 jit_solution(3634078507606203532)
XLA Ops:
  0.0 11.5 %all-to-all-start = ((bf16[128,2,128]{2,1,0:T(2,128)(2,1)}), bf16[128,2,128]{2,1,0:T(2,128)(2,1)S(1)}, u32[]{:S(2)}, u32[]{:S(2)}) async-start(bf16[128,2,128]{2,1,0:T(2,128)(2,1)} %bitcast.14), calls=%async_computation | async-start | bytes 131072 | tf_op jit(solution)/shard_map/all_to_all | solution.py:341
  11.5 1.0 %copy.13.a_rate = f32[6,128,16]{2,1,0:T(8,128)S(1)} copy(f32[6,128,16]{1,2,0:T(8,128)} %param.19) | data formatting | bytes 98304 | tf_op args[8]
  12.5 1.0 %copy.12.x_w = bf16[6,128,36]{2,1,0:T(8,128)(2,1)S(1)} copy(bf16[6,128,36]{1,2,0:T(8,128)(2,1)} %param.16) | data formatting | bytes 110592 | tf_op args[5]
  13.5 0.8 %copy.14.out_w = bf16[128,64]{1,0:T(8,128)(2,1)S(1)} copy(bf16[128,64]{0,1:T(8,128)(2,1)} %param.21) | data formatting | bytes 32768 | tf_op args[10]
  14.3 0.0 copy-start
  14.3 0.8 %copy-done = bf16[64,256]{1,0:T(8,128)(2,1)S(1)} copy-done((bf16[64,256]{1,0:T(8,128)(2,1)S(1)}, bf16[64,256]{1,0:T(8,128)(2,1)}, u32[]{:S(2)}) %copy-start) | copy-done | bytes 32792
  15.1 0.0 copy-start.1
  15.1 0.7 %copy-done.1 = f32[6,4,128]{2,1,0:T(4,128)S(1)} copy-done((f32[6,4,128]{2,1,0:T(4,128)S(1)}, f32[6,4,128]{2,1,0:T(4,128)}, u32[]{:S(2)}) %copy-start.1) | copy-done | bytes 12312
  15.8 0.0 copy-start.2
  15.8 0.7 %copy-done.2 = f32[6,4,128]{2,1,0:T(4,128)S(1)} copy-done((f32[6,4,128]{2,1,0:T(4,128)S(1)}, f32[6,4,128]{2,1,0:T(4,128)}, u32[]{:S(2)}) %copy-start.2) | copy-done | bytes 12312
  16.5 0.0 copy-start.3
  16.5 0.7 %copy-done.3 = f32[6,128]{1,0:T(8,128)S(1)} copy-done((f32[6,128]{1,0:T(8,128)S(1)}, f32[6,128]{1,0:T(8,128)}, u32[]{:S(2)}) %copy-start.3) | copy-done | bytes 3096
  17.2 0.0 copy-start.4
  17.2 0.7 %copy-done.4 = f32[6,128]{1,0:T(8,128)S(1)} copy-done((f32[6,128]{1,0:T(8,128)S(1)}, f32[6,128]{1,0:T(8,128)}, u32[]{:S(2)}) %copy-start.4) | copy-done | bytes 3096
  17.9 0.0 copy-start.5
  17.9 0.7 %copy-done.5 = f32[6,128]{1,0:T(8,128)S(1)} copy-done((f32[6,128]{1,0:T(8,128)S(1)}, f32[6,128]{1,0:T(8,128)}, u32[]{:S(2)}) %copy-start.5) | copy-done | bytes 3096
  18.6 0.0 copy-start.6
  18.6 0.7 %copy-done.6 = f32[64]{0:T(128)S(1)} copy-done((f32[64]{0:T(128)S(1)}, f32[64]{0:T(128)}, u32[]{:S(2)}) %copy-start.6) | copy-done | bytes 280
  19.2 3.6 %prepare.1 = (f32[6,27,32,128]{3,2,1,0:T(8,128)S(1)}, bf16[64,256]{1,0:T(8,128)(2,1)S(1)}, bf16[6,40,128]{2,1,0:T(8,128)(2,1)S(1)}, bf16[4,2,32,128]{3,2,1,0:T(8,128)(2,1)S(1)}, f32[1,128]{1,0:T(1,128)S(1)}) custom-call(bf16[64,256]{1,0:T(8,128)(2,1)S(1)} %copy-done, f32[6,4,128]{2,1,0:T(4,128)S(1)} %copy-done.1, f32[6,128]{1,0:T(8,128)S(1)} %copy-done.3, ...), custom_call_target="tpu_custom_call" | custom-call | tf_op jit(solution)/shard_map/prepare/pallas_call | solution.py:309
  22.8 0.0 copy-start.7
  22.8 0.0 all-to-all-done
  22.8 8.2 %planes.1 = bf16[256,128]{1,0:T(8,128)(2,1)} custom-call(bf16[256,128]{1,0:T(8,128)(2,1)S(1)} %bitcast.12, f32[6,27,32,128]{3,2,1,0:T(8,128)S(1)} %get-tuple-element.10.table, bf16[64,256]{1,0:T(8,128)(2,1)S(1)} %get-tuple-element.11.lhsq_ref, bf16[6,40,128]{2,1,0:T(8,128)(2,1)S(1)} %get-tuple-element.12.xp, ...), custom_call_target="tpu_custom_call" | custom-call | tf_op jit(solution)/shard_map/planes/pallas_call | solution.py:315
  31.0 9.8 %all-to-all-start.1 = ((bf16[128,2,128]{2,1,0:T(2,128)(2,1)}), bf16[128,2,128]{2,1,0:T(2,128)(2,1)S(1)}, u32[]{:S(2)}, u32[]{:S(2)}) async-start(bf16[128,2,128]{2,1,0:T(2,128)(2,1)} %bitcast.5), calls=%async_computation.1 | async-start | bytes 131072 | tf_op jit(solution)/shard_map/all_to_all | solution.py:346
  40.8 0.0 copy-done.7
  40.8 0.1 reshape_reshape.3.values
  40.8 7.2 %z_lines.1 = f32[256,128]{1,0:T(8,128)S(1)} custom-call(bf16[256,128]{1,0:T(8,128)(2,1)S(1)} %reshape_reshape.3.values, f32[6,27,32,128]{3,2,1,0:T(8,128)S(1)} %get-tuple-element.10.table, bf16[64,256]{1,0:T(8,128)(2,1)S(1)} %get-tuple-element.11.lhsq_ref, bf16[6,40,128]{2,1,0:T(8,128)(2,1)S(1)} %get-tuple-element.12.xp, ...), custom_call_target="tpu_custom_call" | custom-call | tf_op jit(solution)/shard_map/z_lines/pallas_call | solution.py:327
  48.0 2.6 %all-to-all-done.1 = bf16[128,2,128]{2,1,0:T(2,128)(2,1)S(1)} async-done(((bf16[128,2,128]{2,1,0:T(2,128)(2,1)}), bf16[128,2,128]{2,1,0:T(2,128)(2,1)S(1)}, u32[]{:S(2)}, u32[]{:S(2)}) %all-to-all-start.1) | async-done | bytes 65568 | tf_op jit(solution)/shard_map/all_to_all | solution.py:346
  50.6 0.7 %fusion = bf16[1,2,16384]{2,1,0:T(2,128)(2,1)} fusion(f32[128,2,128]{2,1,0:T(2,128)S(1)} %bitcast.11, bf16[128,2,128]{2,1,0:T(2,128)(2,1)S(1)} %all-to-all-done.1), kind=kLoop, calls=%fused_computation.1 | loop fusion | flops 98304 | bytes 262144 | tf_op jit(solution)/shard_map/reshape | solution.py:349
Async XLA Ops:
  0.0 22.8 %all-to-all-start = ((bf16[128,2,128]{2,1,0:T(2,128)(2,1)}), bf16[128,2,128]{2,1,0:T(2,128)(2,1)S(1)}, u32[]{:S(2)}, u32[]{:S(2)}) async-start(bf16[128,2,128]{2,1,0:T(2,128)(2,1)} %bitcast.14), calls=%async_computation | async-start | bytes 131072 | tf_op jit(solution)/shard_map/all_to_all | solution.py:341
  14.3 0.8 %copy-start = (bf16[64,256]{1,0:T(8,128)(2,1)S(1)}, bf16[64,256]{1,0:T(8,128)(2,1)}, u32[]{:S(2)}) copy-start(bf16[64,256]{1,0:T(8,128)(2,1)} %in_w.1) | copy-start | bytes 98308
  15.1 0.7 %copy-start.1 = (f32[6,4,128]{2,1,0:T(4,128)S(1)}, f32[6,4,128]{2,1,0:T(4,128)}, u32[]{:S(2)}) copy-start(f32[6,4,128]{2,1,0:T(4,128)} %conv_w.1) | copy-start | bytes 36868
  15.8 0.7 %copy-start.2 = (f32[6,4,128]{2,1,0:T(4,128)S(1)}, f32[6,4,128]{2,1,0:T(4,128)}, u32[]{:S(2)}) copy-start(f32[6,4,128]{2,1,0:T(4,128)} %dt_w.1) | copy-start | bytes 36868
  16.5 0.7 %copy-start.3 = (f32[6,128]{1,0:T(8,128)S(1)}, f32[6,128]{1,0:T(8,128)}, u32[]{:S(2)}) copy-start(f32[6,128]{1,0:T(8,128)} %conv_b.1) | copy-start | bytes 9220
  17.2 0.7 %copy-start.4 = (f32[6,128]{1,0:T(8,128)S(1)}, f32[6,128]{1,0:T(8,128)}, u32[]{:S(2)}) copy-start(f32[6,128]{1,0:T(8,128)} %dt_b.1) | copy-start | bytes 9220
  17.9 0.7 %copy-start.5 = (f32[6,128]{1,0:T(8,128)S(1)}, f32[6,128]{1,0:T(8,128)}, u32[]{:S(2)}) copy-start(f32[6,128]{1,0:T(8,128)} %skip.1) | copy-start | bytes 9220
  18.6 0.7 %copy-start.6 = (f32[64]{0:T(128)S(1)}, f32[64]{0:T(128)}, u32[]{:S(2)}) copy-start(f32[64]{0:T(128)} %param.12) | copy-start | bytes 772
  22.8 18.0 %copy-start.7 = (bf16[1,2,16384]{2,1,0:T(2,128)(2,1)S(1)}, bf16[1,2,16384]{2,1,0:T(2,128)(2,1)}, u32[]{:S(2)}) copy-start(bf16[1,2,16384]{2,1,0:T(2,128)(2,1)} %param.11) | copy-start | bytes 196612
  31.0 19.6 %all-to-all-start.1 = ((bf16[128,2,128]{2,1,0:T(2,128)(2,1)}), bf16[128,2,128]{2,1,0:T(2,128)(2,1)S(1)}, u32[]{:S(2)}, u32[]{:S(2)}) async-start(bf16[128,2,128]{2,1,0:T(2,128)(2,1)} %bitcast.5), calls=%async_computation.1 | async-start | bytes 131072 | tf_op jit(solution)/shard_map/all_to_all | solution.py:346

commit v2 on v1

v2 whole, which is shorter than its diff:
```python
import math

import jax
import jax.numpy as jnp
from jax import lax
from jax.experimental import pallas as pl
from jax.experimental.pallas import tpu as pltpu
from jax.sharding import PartitionSpec as P

C = 64
E = 128
N = 16
R = 4
K = 4
PAD = 8
CW, CB, DB, SK, VEC = 0, 4, 5, 6, 8
Q = 4
EQ = E // Q
STEPS = 16
LINES = 32
A0, CW0, DW0, CB0, DB0, SK0, ROWS = 0, 16, 20, 24, 25, 26, 32
LN2 = math.log(2.0)
LOG2E = 1.0 / LN2
F32 = jnp.float32
BF16 = jnp.bfloat16
HIGHEST = lax.Precision.HIGHEST
NT = (((1,), (1,)), ((), ()))
TN = (((0,), (0,)), ((), ()))
PARAMS = pltpu.CompilerParams(vmem_limit_bytes=48 * 1024 * 1024)


def iota(shape, axis):
    return lax.broadcasted_iota(jnp.int32, shape, axis)


def silu(x):
    half = 0.5 * x
    return half * (1.0 + jnp.tanh(half))


def softplus2(x):
    tail = jnp.exp2(-jnp.abs(x))
    return jnp.maximum(x, 0.0) + jnp.where(tail < 1e-4, tail * LOG2E, jnp.log2(1.0 + tail))


def prepare_kernel(*refs):
    given, (vec, rate_far, w_step, w_in, w_out, gain2, swap), (table, lhsq, xp, wo) = refs[:10], refs[10:17], refs[17:21]
    here, sem = refs[21:31], refs[31]
    copies = [pltpu.make_async_copy(a, b, sem.at[i]) for i, (a, b) in enumerate(zip(given, here))]
    for copy in copies:
        copy.start()
    for copy in copies:
        copy.wait()
    in_w, conv_w, conv_b, x_w, dt_w, dt_b, rate, skip, out_w, gain = here
    row, column = iota((R + 2 * N, E), 0), iota((R + 2 * N, E), 1)
    pick = (row == column % (2 * N) + R).astype(F32)
    for d in range(2, 6):
        vec[d, CW : CW + K] = conv_w[d]
        vec[d, CB : CB + 1] = conv_b[d : d + 1, :]
        vec[d, DB : DB + 1] = dt_b[d : d + 1, :] * LOG2E
        vec[d, SK : SK + 1] = skip[d : d + 1, :]
        vec[d, SK + 1 :] = jnp.zeros((1, E), F32)
        given_w = x_w[d].astype(F32)
        both = lax.dot_general(given_w[:R], dt_w[d] * LOG2E, TN, precision=HIGHEST, preferred_element_type=F32)
        high = both.astype(BF16)
        w_step[d, 0:E, 0:E] = high
        w_step[d, E:, 0:E] = (both - high.astype(F32)).astype(BF16)
        w_step[d, 0:E, E:] = lax.dot_general(given_w, pick, TN, preferred_element_type=F32).astype(BF16)
        w_step[d, E:, E:] = jnp.zeros((E, E), BF16)
    row, column = iota((256, 256), 0), iota((256, 256), 1)
    swap[...] = (column == row % 16 * 16 + row // 16).astype(BF16)
    turned = jnp.concatenate([-rate[2 + i] for i in range(4)], axis=0).T
    high = turned.astype(BF16)
    both = jnp.concatenate([high, (turned - high.astype(F32)).astype(BF16)], axis=1)
    row, column = iota((8 * N, E), 0), iota((8 * N, E), 1)
    for n in range(N):
        chosen = ((row % N == n) & (row // N % 4 == column // 32)).astype(BF16)
        rate_far[n] = jnp.dot(both, chosen, preferred_element_type=F32)
    weight = in_w[...]
    zero = jnp.zeros((C, E), BF16)
    inner, gate = weight[:, :E], weight[:, E:]
    w_in[0:C] = jnp.concatenate([inner, zero, gate, zero], axis=1)
    w_in[C:] = jnp.concatenate([zero, inner, zero, gate], axis=1)
    turned = out_w[...].astype(F32)
    wide = jnp.concatenate([turned, turned], axis=0).T
    low_half = iota((E, 2 * C), 1) < C
    w_out[0:E] = jnp.where(low_half, wide, 0.0).astype(BF16)
    w_out[E:] = jnp.where(low_half, 0.0, wide).astype(BF16)
    gain2[...] = jnp.concatenate([gain[...], gain[...]], axis=1)
    mask = ((iota((EQ, E), 1) % EQ) == iota((EQ, E), 0)).astype(BF16)
    same = (iota((2 * E, E), 0) % E // EQ == iota((2 * E, E), 1) // EQ).astype(BF16)
    row, column = iota((40, 36), 0), iota((40, 36), 1)
    pick = (column == jnp.where(row < 2 * N, row + R, row - 2 * N)) & (row < 2 * N + R)
    pick = pick.astype(BF16)
    for d in range(2):
        rows = jnp.concatenate(
            [
                rate[d] * (-LOG2E),
                conv_w[d],
                dt_w[d],
                conv_b[d : d + 1, :],
                dt_b[d : d + 1, :],
                skip[d : d + 1, :],
                jnp.zeros((5, E), F32),
            ],
            axis=0,
        )
        high = rows.astype(BF16)
        rest = (rows - high.astype(F32)).astype(BF16)
        spread = jnp.concatenate(
            [(part[:, None, :] * mask[None]).reshape(ROWS * EQ, E) for part in (high, rest)], axis=1
        )
        table[d] = jnp.dot(spread, same, preferred_element_type=F32).reshape(ROWS, EQ, E)
        xp[d] = jnp.dot(pick, x_w[d], preferred_element_type=F32).astype(BF16)
    turned = in_w[...].astype(F32).T
    for part in range(2):
        blocks = [turned[part * E + q * EQ : part * E + (q + 1) * EQ] for q in range(Q)]
        lhsq[part * EQ : (part + 1) * EQ, :] = jnp.concatenate(blocks, axis=1).astype(BF16)
    for q in range(Q):
        for half in range(2):
            wo[q, half] = w_out[half * E + q * EQ : half * E + (q + 1) * EQ, :]


def enter(values, gain2, w_in):
    low = iota(values.shape, 1) < C
    squares = values * values
    first = jnp.sum(jnp.where(low, squares, 0.0), axis=1, keepdims=True) * (1.0 / C)
    second = jnp.sum(jnp.where(low, 0.0, squares), axis=1, keepdims=True) * (1.0 / C)
    scale = jnp.where(low, lax.rsqrt(first + 1e-05), lax.rsqrt(second + 1e-05))
    normed = (values * scale * gain2).astype(BF16)
    both = jnp.dot(normed, w_in, preferred_element_type=F32)
    inner = [both[:, h * E : (h + 1) * E].astype(BF16).astype(F32) for h in range(2)]
    gates = [silu(both[:, (2 + h) * E : (3 + h) * E]) for h in range(2)]
    return inner, gates


def leave(first, second, w_out):
    hidden = jnp.concatenate([first.astype(BF16), second.astype(BF16)], axis=1)
    return jnp.dot(hidden, w_out, preferred_element_type=F32)


def step_inputs(taps, vec, w_step):
    pre = vec[CB : CB + 1, :]
    for k in range(K):
        pre = pre + vec[CW + k : CW + k + 1, :] * taps[k]
    act = silu(pre).astype(BF16)
    both = jnp.dot(jnp.concatenate([act, act], axis=1), w_step, preferred_element_type=F32)
    return act.astype(F32), softplus2(both[:, :E] + vec[DB : DB + 1, :]), both[:, E:]


def tree_sum(terms):
    while len(terms) > 1:
        terms = [terms[i] + terms[i + 1] for i in range(0, len(terms), 2)]
    return terms[0]


def plane_kernel(values, vec, rate_far, w_step, w_in, w_out, gain2, swap, out, lines_s, gate_s, step_s, fresh_s, sel_s, step_t, fresh_t, sel_t, y_s, sum_s):
    inner, gates = enter(values[...].astype(F32), gain2[...], w_in[...])
    swapped = jnp.dot(swap[...], jnp.concatenate(inner, axis=1).astype(BF16), preferred_element_type=F32)
    zero = jnp.zeros((96, E), F32)
    for axis in range(2):
        lines_s[axis, 0:96, :] = zero
        lines_s[axis, 608:704, :] = zero
    for h in range(2):
        gate_s[h] = gates[h]
        for i in range(16):
            first = 96 + i * 32 + h * 16
            lines_s[1, first : first + 16, :] = inner[h][i * 16 : (i + 1) * 16]
            lines_s[0, first : first + 16, :] = swapped[i * 16 : (i + 1) * 16, h * E : (h + 1) * E]

    for axis in range(2):
        total = None
        for d in range(2):
            index = 2 + 2 * axis + d
            firsts = [32 * (k if d == 0 else 6 - k) for k in range(K)]
            taps = [lines_s[axis, first : first + 512, :] for first in firsts]
            act, step, sel = step_inputs(taps, vec[index], w_step[index])
            direct = vec[index, SK : SK + 1, :] * act
            total = direct if total is None else total + direct
            fresh = step * act
            rows = slice(axis * 64 + d * 32, axis * 64 + d * 32 + 32)
            for s in range(16):
                t = s if d == 0 else 15 - s
                lanes = slice(s % 4 * 32, s % 4 * 32 + 32)
                step_s[s, rows, :] = step[t * 32 : (t + 1) * 32]
                fresh_s[s, rows, :] = fresh[t * 32 : (t + 1) * 32]
                sel_s[s // 4, rows, lanes] = sel[t * 32 : (t + 1) * 32, lanes]
        sum_s[axis] = total

    for s in range(16):
        step_t[s] = step_s[s].T
        fresh_t[s] = fresh_s[s].T
        if s % 4 == 0:
            sel_t[s * 32 : s * 32 + 128, :] = sel_s[s // 4].T

    def group(g, carry):
        rows = pl.ds(pl.multiple_of(g * 8, 8), 8)
        rates = [rate_far[n, rows, :] for n in range(N)]
        state = None
        for s in range(16):
            step = step_t[s, rows, :]
            fresh = fresh_t[s, rows, :]
            following = []
            total = [None, None]
            for n in range(N):
                at = s * 32 + n
                new = fresh * sel_t[at : at + 1, :]
                if state is not None:
                    new = new + jnp.exp2(step * rates[n]) * state[n]
                following.append(new)
                term = new * sel_t[at + N : at + N + 1, :]
                total[n % 2] = term if total[n % 2] is None else total[n % 2] + term
            state = following
            y_s[s, rows, :] = total[0] + total[1]
        return carry

    lax.fori_loop(0, 16, group, 0)
    turned = [y_s[s].T for s in range(16)]
    sums = []
    for axis in range(2):
        rows = []
        for t in range(16):
            both = turned[t][axis * 64 : axis * 64 + 32] + turned[15 - t][axis * 64 + 32 : axis * 64 + 64]
            rows.append(sum_s[axis, t * 32 : (t + 1) * 32, :] + both * LN2)
        sums.append(rows)
    halves = [jnp.concatenate([row[h * 16 : (h + 1) * 16] for row in sums[0]], axis=0).astype(BF16) for h in range(2)]
    along_y = jnp.dot(swap[...], jnp.concatenate(halves, axis=1), preferred_element_type=F32)
    hidden = []
    for h in range(2):
        along_x = jnp.concatenate([row[h * 16 : (h + 1) * 16] for row in sums[1]], axis=0)
        hidden.append((along_y[:, h * E : (h + 1) * E] + along_x) * gate_s[h])
    out[...] = leave(hidden[0], hidden[1], w_out[...]).astype(BF16)


def z_softplus(x):
    tail = jnp.exp2(jnp.abs(x) * (-LOG2E))
    return jnp.maximum(x, 0.0) + jnp.where(tail < 1e-4, tail, jnp.log(1.0 + tail))


def normalise(values, gain2, plain, rolled):
    low = iota(values.shape, 1) < C
    squares = values * values
    first = jnp.sum(jnp.where(low, squares, 0.0), axis=1, keepdims=True) * (1.0 / C)
    second = jnp.sum(jnp.where(low, 0.0, squares), axis=1, keepdims=True) * (1.0 / C)
    scale = jnp.where(low, lax.rsqrt(first + 1e-05), lax.rsqrt(second + 1e-05))
    normed = (values * scale * gain2).astype(BF16).astype(F32)
    plain[...] = normed
    rolled[...] = pltpu.roll(normed, C, 1)


def project(blocks, lhsq):
    half = jnp.concatenate(blocks, axis=0)
    zero = jnp.zeros_like(half)
    rows = jnp.concatenate(
        [jnp.concatenate([half, zero], axis=1), jnp.concatenate([zero, half], axis=1)], axis=0
    ).astype(BF16)
    both = lax.dot_general(lhsq, rows, NT, preferred_element_type=F32)
    return both[:EQ].astype(BF16).astype(F32), both[EQ:]


def z_step(d, index, neighbours, table, xp, quarter, act_s, sel_s, step_s, fresh_s):
    pre = table[index, CB0]
    for k in range(K):
        if neighbours[k] is not None:
            pre = pre + table[index, CW0 + k] * neighbours[k]
    act = silu(pre).astype(BF16).astype(F32)
    spread = jnp.concatenate([jnp.where(quarter == q, act, 0.0) for q in range(Q)], axis=0).astype(BF16)
    sel = jnp.dot(xp[index], spread, preferred_element_type=F32)
    sel = sel + pltpu.roll(sel, 64, 1)
    sel = sel + pltpu.roll(sel, 32, 1)
    raw = table[index, DB0]
    for r in range(R):
        raw = raw + table[index, DW0 + r] * sel[2 * N + r : 2 * N + r + 1, :]
    step = z_softplus(raw)
    return act, sel, step


def scan_group(index, d, rows, start, table, sel_s, step_s, fresh_s, y_s):
    rates = [table[index, A0 + n, rows, :] for n in range(N)]
    state = start
    for s in range(STEPS):
        t = s if d == 0 else STEPS - 1 - s
        step = step_s[d, t, rows, :]
        fresh = fresh_s[d, t, rows, :]
        total = [None, None]
        following = []
        for n in range(N):
            new = fresh * sel_s[d, t, n : n + 1, :]
            if state is not None:
                new = new + jnp.exp2(step * rates[n]) * state[n]
            following.append(new)
            term = new * sel_s[d, t, N + n : N + n + 1, :]
            total[n % 2] = term if total[n % 2] is None else total[n % 2] + term
        state = following
        y_s[t, rows, :] = y_s[t, rows, :] + (total[0] + total[1])
    return state


def gated_rows(y_s, gate_s, turned_s):
    for t in range(STEPS):
        turned_s[t] = (y_s[t] * gate_s[t]).T


def line_inputs_kernel(values, table, lhsq_ref, xp, gain2, gate_s, sel_s, step_s, fresh_s, y_s, plain, rolled, inner_s):
    normalise(values[...].astype(F32), gain2[...], plain, rolled)
    lane = iota((EQ, E), 1)
    quarter = lane // LINES
    chunk = lane % STEPS
    low = iota((STEPS, 2 * C), 1) < C
    lhsq = lhsq_ref[...]
    for t in range(STEPS):
        blocks = []
        for half in range(2):
            for y in range(2):
                where = pl.ds(y * 128 + t // 2, STEPS, stride=8)
                rows = plain[where, :] if t % 2 == half else rolled[where, :]
                blocks.append(jnp.where(low, rows, 0.0) if half == 0 else jnp.where(low, 0.0, rows))
        inner, gate = project(blocks, lhsq)
        inner_s[t] = inner
        gate_s[t] = silu(gate)
    for d in range(2):
        edge = (chunk >= 1) if d == 0 else (chunk < STEPS - 1)
        for t in range(STEPS):
            near = []
            for k in range(K):
                p = t - 3 + k if d == 0 else t + 3 - k
                if 0 <= p < STEPS:
                    near.append(inner_s[p])
                else:
                    moved = pltpu.roll(inner_s[p % STEPS], 1 if d == 0 else E - 1, 1)
                    near.append(jnp.where(edge, moved, 0.0))
            act, sel, step = z_step(d, d, near, table, xp, quarter, None, sel_s, step_s, fresh_s)
            sel_s[d, t] = sel
            step_s[d, t] = step
            fresh_s[d, t] = step * act
            direct = table[d, SK0] * act
            y_s[t] = direct if d == 0 else y_s[t] + direct


def line_scan_kernel(table, wo, gate_s, sel_s, step_s, fresh_s, direct_s, out, y_s, turned_s):
    far_off = 1e4
    y_s[...] = direct_s[...]

    def group(g, carry):
        rows = pl.ds(pl.multiple_of(g * 8, 8), 8)
        place = iota((8, E), 1) % STEPS
        for d in range(2):
            rates = [table[d, A0 + n, rows, :] for n in range(N)]
            ends = None
            whole = None
            for s in range(STEPS):
                t = s if d == 0 else STEPS - 1 - s
                step = step_s[d, t, rows, :]
                fresh = fresh_s[d, t, rows, :]
                whole = step if whole is None else whole + step
                following = []
                for n in range(N):
                    new = fresh * sel_s[d, t, n : n + 1, :]
                    if ends is not None:
                        new = new + jnp.exp2(step * rates[n]) * ends[n]
                    following.append(new)
                ends = following
            before = place if d == 0 else STEPS - 1 - place

            def moved(x, k, d=d):
                return pltpu.roll(x, k if d == 0 else E - k, 1)

            def kept(k, x, before=before):
                return jnp.where(before >= k, x, far_off)

            one = moved(whole, 1)
            two = one + moved(whole, 2)
            three = two + moved(whole, 3)
            four = three + moved(whole, 4)
            eight = four + moved(four, 4)
            twelve = eight + moved(four, 8)
            spans = [kept(2, one), kept(3, two), kept(4, three)]
            wide = [kept(4, four), kept(8, eight), kept(12, twelve)]
            start = []
            for n in range(N):
                sums = jnp.where(before >= 1, moved(ends[n], 1), 0.0)
                for k in range(3):
                    sums = sums + jnp.exp2(spans[k] * rates[n]) * moved(ends[n], k + 2)
                start.append(sums)
            for n in range(N):
                sums = start[n]
                for k in range(3):
                    sums = sums + jnp.exp2(wide[k] * rates[n]) * moved(start[n], 4 * k + 4)
                start[n] = sums
            scan_group(d, d, rows, start, table, sel_s, step_s, fresh_s, y_s)
        return carry

    lax.fori_loop(0, EQ // 8, group, 0)
    gated_rows(y_s, gate_s, turned_s)
    near = None
    for q in range(Q):
        for half in range(2):
            steps = [turned_s[2 * p + half, q * LINES : (q + 1) * LINES, :] for p in range(8)]
            lhs = jnp.concatenate(steps, axis=0).astype(BF16)
            part = jnp.dot(lhs, wo[q, half], preferred_element_type=F32)
            near = part if near is None else near + part
    for p in range(8):
        for y in range(2):
            first = p * LINES + y * STEPS
            out[pl.ds(2 * p + y, STEPS, stride=16), :] = near[first : first + STEPS]


def vmem(count):
    return [pl.BlockSpec(memory_space=pltpu.VMEM)] * count


def prepare(*weights):
    shapes = [
        jax.ShapeDtypeStruct((6, VEC, E), F32),
        jax.ShapeDtypeStruct((N, E, E), F32),
        jax.ShapeDtypeStruct((6, 2 * E, 2 * E), BF16),
        jax.ShapeDtypeStruct((2 * C, 4 * E), BF16),
        jax.ShapeDtypeStruct((2 * E, 2 * C), BF16),
        jax.ShapeDtypeStruct((1, 2 * C), F32),
        jax.ShapeDtypeStruct((256, 256), BF16),
        jax.ShapeDtypeStruct((2, ROWS, EQ, E), F32),
        jax.ShapeDtypeStruct((2 * EQ, Q * C), BF16),
        jax.ShapeDtypeStruct((2, 40, E), BF16),
        jax.ShapeDtypeStruct((Q, 2, EQ, 2 * C), BF16),
    ]
    ready = pl.pallas_call(
        prepare_kernel,
        out_shape=shapes,
        in_specs=[pl.BlockSpec(memory_space=pl.ANY)] * 10,
        out_specs=vmem(11),
        scratch_shapes=[pltpu.VMEM(w.shape, w.dtype) for w in weights] + [pltpu.SemaphoreType.DMA((10,))],
        compiler_params=PARAMS,
        name="prepare",
    )(*[pltpu.with_memory_space_constraint(w, pltpu.HBM) for w in weights])
    return ready[:7], (*ready[7:], ready[5])


def planes(values, ready):
    return pl.pallas_call(
        plane_kernel,
        out_shape=jax.ShapeDtypeStruct((256, 2 * C), BF16),
        in_specs=vmem(8),
        out_specs=vmem(1)[0],
        scratch_shapes=[
            pltpu.VMEM((2, 704, E), F32),
            pltpu.VMEM((2, 256, E), F32),
            pltpu.VMEM((16, E, E), F32),
            pltpu.VMEM((16, E, E), F32),
            pltpu.VMEM((4, E, E), F32),
            pltpu.VMEM((16, E, E), F32),
            pltpu.VMEM((16, E, E), F32),
            pltpu.VMEM((16 * 2 * N, E), F32),
            pltpu.VMEM((16, E, E), F32),
            pltpu.VMEM((2, 512, E), F32),
        ],
        compiler_params=PARAMS,
        name="planes",
    )(values, *ready)


def z_inputs(values, ready):
    table, lhsq, xp, _, gain2 = ready
    return pl.pallas_call(
        line_inputs_kernel,
        out_shape=[
            jax.ShapeDtypeStruct((STEPS, EQ, E), F32),
            jax.ShapeDtypeStruct((2, STEPS, 40, E), F32),
            jax.ShapeDtypeStruct((2, STEPS, EQ, E), F32),
            jax.ShapeDtypeStruct((2, STEPS, EQ, E), F32),
            jax.ShapeDtypeStruct((STEPS, EQ, E), F32),
        ],
        in_specs=vmem(5),
        out_specs=vmem(5),
        scratch_shapes=[pltpu.VMEM((256, E), F32), pltpu.VMEM((256, E), F32), pltpu.VMEM((STEPS, EQ, E), F32)],
        compiler_params=PARAMS,
        name="z_inputs",
    )(values, table, lhsq, xp, gain2)


def z_lines(given, ready):
    table, _, _, wo, _ = ready
    return pl.pallas_call(
        line_scan_kernel,
        out_shape=jax.ShapeDtypeStruct((256, 2 * C), F32),
        in_specs=vmem(7),
        out_specs=vmem(1)[0],
        scratch_shapes=[pltpu.VMEM((STEPS, EQ, E), F32), pltpu.VMEM((STEPS, E, EQ), F32)],
        compiler_params=PARAMS,
        name="z_lines",
    )(table, wo, *given)


def local(voxels, norm_gain, in_weight, conv_weight, conv_bias, x_weight, dt_weight, dt_bias, a_rate, skip_gain, out_weight):
    pairs = voxels.reshape(2, 128, 2 * C)
    sent = pairs.transpose(1, 0, 2)
    arrived = lax.all_to_all(sent, ("row", "col"), split_axis=0, concat_axis=0, tiled=True)
    ready, z_ready = prepare(
        in_weight,
        conv_weight,
        conv_bias,
        x_weight.transpose(0, 2, 1),
        dt_weight,
        dt_bias,
        a_rate.transpose(0, 2, 1),
        skip_gain,
        out_weight.T,
        norm_gain.reshape(1, C),
    )
    given = z_inputs(pairs.reshape(256, 2 * C), z_ready)
    far = planes(arrived.reshape(256, 2 * C), ready)
    returned = lax.all_to_all(far.reshape(128, 2, 2 * C), ("row", "col"), split_axis=0, concat_axis=0, tiled=True)
    near = z_lines(given, z_ready)
    mixed = (near.reshape(128, 2, 2 * C) + returned.astype(F32)).astype(BF16)
    return mixed.transpose(1, 0, 2).reshape(1, 2, 128 * 2 * C)


def solution(mesh):
    in_specs = (P("row", "col", None),) + (P(),) * 10
    return jax.shard_map(local, mesh=mesh, in_specs=in_specs, out_specs=P("row", "col", None), check_vma=False)
```

time: 51.8 us -> 43.1 us (0.83)
  waiting for transfers between devices: 2.57 us -> 10.9 us
  local copies, waits for them, and re-layouts: 7.75 us -> 0.06 us
  starting transfers between devices: 21.3 us -> 15.6 us
  Pallas kernels: 18.9 us -> 15.6 us
    all_to_all x1, waiting for transfers between devices: 0.01 us -> 7.82 us  [local(): lax.all_to_all(sent, ('row', 'col'), split_axis=0, concat_axis=0, tiled=T...]
    unnamed x19 -> x2, local copies, waits for them, and re-layouts: 7.69 us -> 0.01 us
    all_to_all x1, starting transfers between devices: 9.76 us -> 4.15 us  [local(): lax.all_to_all(far.reshape(128, 2, 2 * C), ('row', 'col'), split_axis=0,...]
    pallas_call x2 -> x3, Pallas kernels: 10.7 us -> 8.67 us  [the longest x1 5.16 us: z_lines(): pl.pallas_call(line_scan_kernel, out_shape=jax.ShapeDtypeStruct((256, 2 *...]
    pallas_call x1, Pallas kernels: 8.18 us -> 6.9 us  [planes(): pl.pallas_call(plane_kernel, out_shape=jax.ShapeDtypeStruct((256, 2 * C),...]
  transfers between devices with their start and end apart: 2 -> 2, of which waited for: 1 -> 2; matrix products, arithmetic and copies ran while one was open for 6% -> 0% of each run, Pallas kernels for 21% -> 20%
where the time goes in v2:
time: 43.1 us; the launch traced here: 42.9 us
  starting transfers between devices  15.6 us (36%)
  Pallas kernels  15.6 us (36%)
  waiting for transfers between devices  10.9 us (25%)
  other arithmetic  0.7 us (2%)
    all_to_all x1, starting transfers between devices, local(): lax.all_to_all(sent, ('row', 'col'), split_axis=0, concat_axis=0, tiled=T...  11.5 us
    all_to_all x1, waiting for transfers between devices, local(): lax.all_to_all(sent, ('row', 'col'), split_axis=0, concat_axis=0, tiled=T...  7.82 us
    pallas_call x1, Pallas kernels, planes(): pl.pallas_call(plane_kernel, out_shape=jax.ShapeDtypeStruct((256, 2 * C),...  6.9 us
    pallas_call x1, Pallas kernels, z_lines(): pl.pallas_call(line_scan_kernel, out_shape=jax.ShapeDtypeStruct((256, 2 *...  5.16 us
    all_to_all x1, starting transfers between devices, local(): lax.all_to_all(far.reshape(128, 2, 2 * C), ('row', 'col'), split_axis=0,...  4.15 us
    all_to_all x1, waiting for transfers between devices, local(): lax.all_to_all(far.reshape(128, 2, 2 * C), ('row', 'col'), split_axis=0,...  3.05 us
    pallas_call x1, Pallas kernels, prepare(): pl.pallas_call(prepare_kernel, out_shape=shapes, in_specs=[pl.BlockSpec(m...  1.98 us
    pallas_call x1, Pallas kernels, z_inputs(): pl.pallas_call(line_inputs_kernel, out_shape=[jax.ShapeDtypeStruct((STEPS...  1.53 us
  transfers between devices with their start and end apart: 2, of which 2 were waited for; matrix products, arithmetic and copies ran while one was open for 0% of the time, Pallas kernels for 20%

profile of v2, /device:TPU:1, one launch (start us, length us, event | category | flops | bytes accessed | tf_op | source)
XLA Modules:
  0.0 42.9 jit_solution(4965835468884875202)
XLA Ops:
  0.0 11.5 %all-to-all-start = ((bf16[128,2,128]{2,1,0:T(2,128)(2,1)}), bf16[128,2,128]{2,1,0:T(2,128)(2,1)S(1)}, u32[]{:S(2)}, u32[]{:S(2)}) async-start(bf16[128,2,128]{2,1,0:T(2,128)(2,1)} %bitcast.16), calls=%async_computation | async-start | bytes 131072 | tf_op jit(solution)/shard_map/all_to_all | solution.py:496
  11.5 2.0 %prepare.1 = (f32[6,8,128]{2,1,0:T(8,128)S(1)}, f32[16,128,128]{2,1,0:T(8,128)S(1)}, bf16[6,256,256]{2,1,0:T(8,128)(2,1)S(1)}, bf16[128,512]{1,0:T(8,128)(2,1)S(...) custom-call(bf16[64,256]{1,0:T(8,128)(2,1)} %refs_0_.1, ...), custom_call_target="tpu_custom_call" | custom-call | tf_op jit(solution)/shard_map/prepare/pallas_call | solution.py:426
  13.5 7.8 %all-to-all-done = bf16[128,2,128]{2,1,0:T(2,128)(2,1)S(1)} async-done(((bf16[128,2,128]{2,1,0:T(2,128)(2,1)}), bf16[128,2,128]{2,1,0:T(2,128)(2,1)S(1)}, u32[]{:S(2)}, u32[]{:S(2)}) %all-to-all-start) | async-done | bytes 65568 | tf_op jit(solution)/shard_map/all_to_all | solution.py:496
  21.3 6.9 %planes.1 = bf16[256,128]{1,0:T(8,128)(2,1)} custom-call(bf16[256,128]{1,0:T(8,128)(2,1)S(1)} %bitcast.15, f32[6,8,128]{2,1,0:T(8,128)S(1)} %get-tuple-element.31.vec, f32[16,128,128]{2,1,0:T(8,128)S(1)} %get-tuple-element.32.rate_far, bf16[6,256,256]{2,1,0:T(8,128)(2,1)S(1)} %get-tuple-element.33.w_step, bf16[128,512]{1,0:T(8,128)(2,1)S(1)} %get-tuple-element.34.w_in, ...), custom_call_target="tpu_custom_call" | custom-call | tf_op jit(solution)/shard_map/planes/pallas_call | solution.py:439
  28.2 0.0 copy-start
  28.2 4.1 %all-to-all-start.1 = ((bf16[128,2,128]{2,1,0:T(2,128)(2,1)}), bf16[128,2,128]{2,1,0:T(2,128)(2,1)S(1)}, u32[]{:S(2)}, u32[]{:S(2)}) async-start(bf16[128,2,128]{2,1,0:T(2,128)(2,1)} %bitcast.8), calls=%async_computation.1 | async-start | bytes 131072 | tf_op jit(solution)/shard_map/all_to_all | solution.py:511
  32.4 0.0 copy-done
  32.4 0.1 reshape_reshape.3.values
  32.4 1.5 %z_inputs.1 = (f32[16,32,128]{2,1,0:T(8,128)S(1)}, f32[2,16,40,128]{3,2,1,0:T(8,128)S(1)}, f32[2,16,32,128]{3,2,1,0:T(8,128)S(1)}, f32[2,16,32,128]{3,2,1,0:T(8,128)S(1)}, f32[16,32,128]{2,1,0:T(8,128)S(1)}) custom-call(bf16[256,128]{1,0:T(8,128)(2,1)S(1)} %reshape_reshape.3.values, f32[2,32,32,128]{3,2,1,0:T(8,128)S(1)} %get-tuple-element.21.table, ...), custom_call_target="tpu_custom_call" | custom-call | tf_op jit(solution)/shard_map/z_inputs/pallas_call | solution.py:463
  34.0 5.2 %z_lines.1 = f32[256,128]{1,0:T(8,128)S(1)} custom-call(f32[2,32,32,128]{3,2,1,0:T(8,128)S(1)} %get-tuple-element.21.table, bf16[4,2,32,128]{3,2,1,0:T(8,128)(2,1)S(1)} %get-tuple-element.22.wo, f32[16,32,128]{2,1,0:T(8,128)S(1)} %get-tuple-element.26.gate_s, f32[2,16,40,128]{3,2,1,0:T(8,128)S(1)} %get-tuple-element.27.sel_s, ...), custom_call_target="tpu_custom_call" | custom-call | tf_op jit(solution)/shard_map/z_lines/pallas_call | solution.py:482
  39.1 3.1 %all-to-all-done.1 = bf16[128,2,128]{2,1,0:T(2,128)(2,1)S(1)} async-done(((bf16[128,2,128]{2,1,0:T(2,128)(2,1)}), bf16[128,2,128]{2,1,0:T(2,128)(2,1)S(1)}, u32[]{:S(2)}, u32[]{:S(2)}) %all-to-all-start.1) | async-done | bytes 65568 | tf_op jit(solution)/shard_map/all_to_all | solution.py:511
  42.2 0.7 %fusion = bf16[1,2,16384]{2,1,0:T(2,128)(2,1)} fusion(f32[128,2,128]{2,1,0:T(2,128)S(1)} %bitcast.14, bf16[128,2,128]{2,1,0:T(2,128)(2,1)S(1)} %all-to-all-done.1), kind=kLoop, calls=%fused_computation.1 | loop fusion | flops 98304 | bytes 262144 | tf_op jit(solution)/shard_map/reshape | solution.py:514
Async XLA Ops:
  0.0 21.3 %all-to-all-start = ((bf16[128,2,128]{2,1,0:T(2,128)(2,1)}), bf16[128,2,128]{2,1,0:T(2,128)(2,1)S(1)}, u32[]{:S(2)}, u32[]{:S(2)}) async-start(bf16[128,2,128]{2,1,0:T(2,128)(2,1)} %bitcast.16), calls=%async_computation | async-start | bytes 131072 | tf_op jit(solution)/shard_map/all_to_all | solution.py:496
  28.2 4.2 %copy-start = (bf16[1,2,16384]{2,1,0:T(2,128)(2,1)S(1)}, bf16[1,2,16384]{2,1,0:T(2,128)(2,1)}, u32[]{:S(2)}) copy-start(bf16[1,2,16384]{2,1,0:T(2,128)(2,1)} %param.11) | copy-start | bytes 196612
  28.2 14.0 %all-to-all-start.1 = ((bf16[128,2,128]{2,1,0:T(2,128)(2,1)}), bf16[128,2,128]{2,1,0:T(2,128)(2,1)S(1)}, u32[]{:S(2)}, u32[]{:S(2)}) async-start(bf16[128,2,128]{2,1,0:T(2,128)(2,1)} %bitcast.8), calls=%async_computation.1 | async-start | bytes 131072 | tf_op jit(solution)/shard_map/all_to_all | solution.py:511

commit v3 on v2

--- a/solution.py
+++ b/solution.py
@@ -55,8 +55,8 @@
     row, column = iota((R + 2 * N, E), 0), iota((R + 2 * N, E), 1)
     pick = (row == column % (2 * N) + R).astype(F32)
     for d in range(2, 6):
-        vec[d, CW : CW + K] = conv_w[d]
-        vec[d, CB : CB + 1] = conv_b[d : d + 1, :]
+        vec[d, CW : CW + K] = conv_w[d] * 0.5
+        vec[d, CB : CB + 1] = conv_b[d : d + 1, :] * 0.5
         vec[d, DB : DB + 1] = dt_b[d : d + 1, :] * LOG2E
         vec[d, SK : SK + 1] = skip[d : d + 1, :]
         vec[d, SK + 1 :] = jnp.zeros((1, E), F32)
@@ -121,17 +121,13 @@
             wo[q, half] = w_out[half * E + q * EQ : half * E + (q + 1) * EQ, :]
 
 
-def enter(values, gain2, w_in):
-    low = iota(values.shape, 1) < C
+def enter(values, gain2):
     squares = values * values
-    first = jnp.sum(jnp.where(low, squares, 0.0), axis=1, keepdims=True) * (1.0 / C)
-    second = jnp.sum(jnp.where(low, 0.0, squares), axis=1, keepdims=True) * (1.0 / C)
-    scale = jnp.where(low, lax.rsqrt(first + 1e-05), lax.rsqrt(second + 1e-05))
-    normed = (values * scale * gain2).astype(BF16)
-    both = jnp.dot(normed, w_in, preferred_element_type=F32)
-    inner = [both[:, h * E : (h + 1) * E].astype(BF16).astype(F32) for h in range(2)]
-    gates = [silu(both[:, (2 + h) * E : (3 + h) * E]) for h in range(2)]
-    return inner, gates
+    high = squares.astype(BF16)
+    rest = (squares - high.astype(F32)).astype(BF16)
+    block = iota((4 * C, 2 * C), 0) % (2 * C) // C == iota((4 * C, 2 * C), 1) // C
+    total = jnp.dot(jnp.concatenate([high, rest], axis=1), block.astype(BF16), preferred_element_type=F32)
+    return (values * lax.rsqrt(total * (1.0 / C) + 1e-05) * gain2).astype(BF16)
 
 
 def leave(first, second, w_out):
@@ -140,10 +136,10 @@
 
 
 def step_inputs(taps, vec, w_step):
-    pre = vec[CB : CB + 1, :]
+    half = vec[CB : CB + 1, :]
     for k in range(K):
-        pre = pre + vec[CW + k : CW + k + 1, :] * taps[k]
-    act = silu(pre).astype(BF16)
+        half = half + vec[CW + k : CW + k + 1, :] * taps[k]
+    act = (half + half * jnp.tanh(half)).astype(BF16)
     both = jnp.dot(jnp.concatenate([act, act], axis=1), w_step, preferred_element_type=F32)
     return act.astype(F32), softplus2(both[:, :E] + vec[DB : DB + 1, :]), both[:, E:]
 
@@ -154,81 +150,89 @@
     return terms[0]
 
 
-def plane_kernel(values, vec, rate_far, w_step, w_in, w_out, gain2, swap, out, lines_s, gate_s, step_s, fresh_s, sel_s, step_t, fresh_t, sel_t, y_s, sum_s):
-    inner, gates = enter(values[...].astype(F32), gain2[...], w_in[...])
-    swapped = jnp.dot(swap[...], jnp.concatenate(inner, axis=1).astype(BF16), preferred_element_type=F32)
+def plane_kernel(values, vec, rate_far, w_step, w_in, w_out, gain2, swap, out, lines_s, normed_s, step_s, fresh_s, sel_s, step_t, fresh_t, sel_t, y_s, direct_s):
+    normed = enter(values[...].astype(F32), gain2[...])
+    normed_s[...] = normed
+    both = jnp.dot(normed, w_in[:, : 2 * E], preferred_element_type=F32).astype(BF16)
+    inner = [both[:, h * E : (h + 1) * E].astype(F32) for h in range(2)]
+    swapped = jnp.dot(swap[...], both, preferred_element_type=F32)
     zero = jnp.zeros((96, E), F32)
     for axis in range(2):
         lines_s[axis, 0:96, :] = zero
         lines_s[axis, 608:704, :] = zero
     for h in range(2):
-        gate_s[h] = gates[h]
         for i in range(16):
             first = 96 + i * 32 + h * 16
             lines_s[1, first : first + 16, :] = inner[h][i * 16 : (i + 1) * 16]
             lines_s[0, first : first + 16, :] = swapped[i * 16 : (i + 1) * 16, h * E : (h + 1) * E]
 
-    for axis in range(2):
-        total = None
-        for d in range(2):
-            index = 2 + 2 * axis + d
-            firsts = [32 * (k if d == 0 else 6 - k) for k in range(K)]
-            taps = [lines_s[axis, first : first + 512, :] for first in firsts]
-            act, step, sel = step_inputs(taps, vec[index], w_step[index])
-            direct = vec[index, SK : SK + 1, :] * act
-            total = direct if total is None else total + direct
-            fresh = step * act
-            rows = slice(axis * 64 + d * 32, axis * 64 + d * 32 + 32)
+    for part in range(4):
+        for axis in range(2):
+            for d in range(2):
+                index = 2 + 2 * axis + d
+                begin = 4 * part if d == 0 else 12 - 4 * part
+                firsts = [32 * (begin + (k if d == 0 else 6 - k)) for k in range(K)]
+                taps = [lines_s[axis, first : first + 128, :] for first in firsts]
+                act, step, sel = step_inputs(taps, vec[index], w_step[index])
+                direct_s[axis, d, begin * 32 : begin * 32 + 128, :] = vec[index, SK : SK + 1, :] * act
+                fresh = step * act
+                rows = slice(axis * 64 + d * 32, axis * 64 + d * 32 + 32)
+                for i in range(4):
+                    t = i if d == 0 else 3 - i
+                    lanes = slice(i * 32, i * 32 + 32)
+                    step_s[4 * part + i, rows, :] = step[t * 32 : (t + 1) * 32]
+                    fresh_s[4 * part + i, rows, :] = fresh[t * 32 : (t + 1) * 32]
+                    sel_s[part, rows, lanes] = sel[t * 32 : (t + 1) * 32, lanes]
+        for s in range(4 * part, 4 * part + 4):
+            step_t[s] = step_s[s].T
+            fresh_t[s] = fresh_s[s].T
+        sel_t[part * 128 : part * 128 + 128, :] = sel_s[part].T
+
+    def group(g, carry):
+        rows = [pl.ds(pl.multiple_of(g * 16 + 8 * i, 8), 8) for i in range(2)]
+        results = []
+        for i in range(2):
+            rates = [rate_far[n, rows[i], :] for n in range(N)]
+            state = None
+            result = []
             for s in range(16):
-                t = s if d == 0 else 15 - s
-                lanes = slice(s % 4 * 32, s % 4 * 32 + 32)
-                step_s[s, rows, :] = step[t * 32 : (t + 1) * 32]
-                fresh_s[s, rows, :] = fresh[t * 32 : (t + 1) * 32]
-                sel_s[s // 4, rows, lanes] = sel[t * 32 : (t + 1) * 32, lanes]
-        sum_s[axis] = total
-
-    for s in range(16):
-        step_t[s] = step_s[s].T
-        fresh_t[s] = fresh_s[s].T
-        if s % 4 == 0:
-            sel_t[s * 32 : s * 32 + 128, :] = sel_s[s // 4].T
-
-    def group(g, carry):
-        rows = pl.ds(pl.multiple_of(g * 8, 8), 8)
-        rates = [rate_far[n, rows, :] for n in range(N)]
-        state = None
+                step = step_t[s, rows[i], :]
+                fresh = fresh_t[s, rows[i], :]
+                following = []
+                total = [None, None]
+                for n in range(N):
+                    at = s * 32 + n
+                    new = fresh * sel_t[at : at + 1, :]
+                    if state is not None:
+                        new = new + jnp.exp2(step * rates[n]) * state[n]
+                    following.append(new)
+                    term = new * sel_t[at + N : at + N + 1, :]
+                    total[n % 2] = term if total[n % 2] is None else total[n % 2] + term
+                state = following
+                result.append(total[0] + total[1])
+            results.append(result)
+        here = pl.ds(pl.multiple_of(g * 16, 16), 16)
         for s in range(16):
-            step = step_t[s, rows, :]
-            fresh = fresh_t[s, rows, :]
-            following = []
-            total = [None, None]
-            for n in range(N):
-                at = s * 32 + n
-                new = fresh * sel_t[at : at + 1, :]
-                if state is not None:
-                    new = new + jnp.exp2(step * rates[n]) * state[n]
-                following.append(new)
-                term = new * sel_t[at + N : at + N + 1, :]
-                total[n % 2] = term if total[n % 2] is None else total[n % 2] + term
-            state = following
-            y_s[s, rows, :] = total[0] + total[1]
+            y_s[s, here, :] = jnp.concatenate([results[0][s], results[1][s]], axis=0).astype(BF16)
         return carry
 
-    lax.fori_loop(0, 16, group, 0)
-    turned = [y_s[s].T for s in range(16)]
+    lax.fori_loop(0, 8, group, 0)
+    gates = silu(jnp.dot(normed_s[...], w_in[:, 2 * E :], preferred_element_type=F32))
+    turned = [y_s[s].T.astype(F32) for s in range(16)]
     sums = []
     for axis in range(2):
         rows = []
         for t in range(16):
             both = turned[t][axis * 64 : axis * 64 + 32] + turned[15 - t][axis * 64 + 32 : axis * 64 + 64]
-            rows.append(sum_s[axis, t * 32 : (t + 1) * 32, :] + both * LN2)
+            here = pl.ds(t * 32, 32)
+            rows.append(direct_s[axis, 0, here, :] + direct_s[axis, 1, here, :] + both * LN2)
         sums.append(rows)
     halves = [jnp.concatenate([row[h * 16 : (h + 1) * 16] for row in sums[0]], axis=0).astype(BF16) for h in range(2)]
     along_y = jnp.dot(swap[...], jnp.concatenate(halves, axis=1), preferred_element_type=F32)
     hidden = []
     for h in range(2):
         along_x = jnp.concatenate([row[h * 16 : (h + 1) * 16] for row in sums[1]], axis=0)
-        hidden.append((along_y[:, h * E : (h + 1) * E] + along_x) * gate_s[h])
+        hidden.append((along_y[:, h * E : (h + 1) * E] + along_x) * gates[:, h * E : (h + 1) * E])
     out[...] = leave(hidden[0], hidden[1], w_out[...]).astype(BF16)
 
 
@@ -443,15 +447,15 @@
         out_specs=vmem(1)[0],
         scratch_shapes=[
             pltpu.VMEM((2, 704, E), F32),
-            pltpu.VMEM((2, 256, E), F32),
+            pltpu.VMEM((256, E), BF16),
             pltpu.VMEM((16, E, E), F32),
             pltpu.VMEM((16, E, E), F32),
             pltpu.VMEM((4, E, E), F32),
             pltpu.VMEM((16, E, E), F32),
             pltpu.VMEM((16, E, E), F32),
             pltpu.VMEM((16 * 2 * N, E), F32),
-            pltpu.VMEM((16, E, E), F32),
-            pltpu.VMEM((2, 512, E), F32),
+            pltpu.VMEM((16, E, E), BF16),
+            pltpu.VMEM((2, 2, 512, E), F32),
         ],
         compiler_params=PARAMS,
         name="planes",

time: 43.1 us -> 42.9 us (level)
  no operation moved by 1% of the time
where the time goes in v3:
time: 42.9 us; the launch traced here: 42.7 us
  starting transfers between devices  15.6 us (36%)
  Pallas kernels  15.3 us (36%)
  waiting for transfers between devices  10.9 us (25%)
  other arithmetic  0.7 us (2%)
    all_to_all x1, starting transfers between devices, local(): lax.all_to_all(sent, ('row', 'col'), split_axis=0, concat_axis=0, tiled=T...  11.5 us
    all_to_all x1, waiting for transfers between devices, local(): lax.all_to_all(sent, ('row', 'col'), split_axis=0, concat_axis=0, tiled=T...  7.82 us
    pallas_call x1, Pallas kernels, planes(): pl.pallas_call(plane_kernel, out_shape=jax.ShapeDtypeStruct((256, 2 * C),...  6.65 us
    pallas_call x1, Pallas kernels, z_lines(): pl.pallas_call(line_scan_kernel, out_shape=jax.ShapeDtypeStruct((256, 2 *...  5.16 us
    all_to_all x1, starting transfers between devices, local(): lax.all_to_all(far.reshape(128, 2, 2 * C), ('row', 'col'), split_axis=0,...  4.15 us
    all_to_all x1, waiting for transfers between devices, local(): lax.all_to_all(far.reshape(128, 2, 2 * C), ('row', 'col'), split_axis=0,...  3.05 us
    pallas_call x1, Pallas kernels, prepare(): pl.pallas_call(prepare_kernel, out_shape=shapes, in_specs=[pl.BlockSpec(m...  1.99 us
    pallas_call x1, Pallas kernels, z_inputs(): pl.pallas_call(line_inputs_kernel, out_shape=[jax.ShapeDtypeStruct((STEPS...  1.53 us
  transfers between devices with their start and end apart: 2, of which 2 were waited for; matrix products, arithmetic and copies ran while one was open for 0% of the time, Pallas kernels for 20%

profile of v3, /device:TPU:1, one launch (start us, length us, event | category | flops | bytes accessed | tf_op | source)
XLA Modules:
  0.0 42.7 jit_solution(16503717296470417699)
XLA Ops:
  0.0 11.5 %all-to-all-start = ((bf16[128,2,128]{2,1,0:T(2,128)(2,1)}), bf16[128,2,128]{2,1,0:T(2,128)(2,1)S(1)}, u32[]{:S(2)}, u32[]{:S(2)}) async-start(bf16[128,2,128]{2,1,0:T(2,128)(2,1)} %bitcast.16), calls=%async_computation | async-start | bytes 131072 | tf_op jit(solution)/shard_map/all_to_all | solution.py:500
  11.5 2.0 %prepare.1 = (f32[6,8,128]{2,1,0:T(8,128)S(1)}, f32[16,128,128]{2,1,0:T(8,128)S(1)}, bf16[6,256,256]{2,1,0:T(8,128)(2,1)S(1)}, bf16[128,512]{1,0:T(8,128)(2,1)S(...) custom-call(bf16[64,256]{1,0:T(8,128)(2,1)} %refs_0_.1, ...), custom_call_target="tpu_custom_call" | custom-call | tf_op jit(solution)/shard_map/prepare/pallas_call | solution.py:430
  13.5 7.8 %all-to-all-done = bf16[128,2,128]{2,1,0:T(2,128)(2,1)S(1)} async-done(((bf16[128,2,128]{2,1,0:T(2,128)(2,1)}), bf16[128,2,128]{2,1,0:T(2,128)(2,1)S(1)}, u32[]{:S(2)}, u32[]{:S(2)}) %all-to-all-start) | async-done | bytes 65568 | tf_op jit(solution)/shard_map/all_to_all | solution.py:500
  21.3 6.7 %planes.1 = bf16[256,128]{1,0:T(8,128)(2,1)} custom-call(bf16[256,128]{1,0:T(8,128)(2,1)S(1)} %bitcast.15, f32[6,8,128]{2,1,0:T(8,128)S(1)} %get-tuple-element.31.vec, f32[16,128,128]{2,1,0:T(8,128)S(1)} %get-tuple-element.32.rate_far, bf16[6,256,256]{2,1,0:T(8,128)(2,1)S(1)} %get-tuple-element.33.w_step, bf16[128,512]{1,0:T(8,128)(2,1)S(1)} %get-tuple-element.34.w_in, ...), custom_call_target="tpu_custom_call" | custom-call | tf_op jit(solution)/shard_map/planes/pallas_call | solution.py:443
  28.0 0.0 copy-start
  28.0 4.2 %all-to-all-start.1 = ((bf16[128,2,128]{2,1,0:T(2,128)(2,1)}), bf16[128,2,128]{2,1,0:T(2,128)(2,1)S(1)}, u32[]{:S(2)}, u32[]{:S(2)}) async-start(bf16[128,2,128]{2,1,0:T(2,128)(2,1)} %bitcast.8), calls=%async_computation.1 | async-start | bytes 131072 | tf_op jit(solution)/shard_map/all_to_all | solution.py:515
  32.1 0.0 copy-done
  32.1 0.1 reshape_reshape.3.values
  32.2 1.5 %z_inputs.1 = (f32[16,32,128]{2,1,0:T(8,128)S(1)}, f32[2,16,40,128]{3,2,1,0:T(8,128)S(1)}, f32[2,16,32,128]{3,2,1,0:T(8,128)S(1)}, f32[2,16,32,128]{3,2,1,0:T(8,128)S(1)}, f32[16,32,128]{2,1,0:T(8,128)S(1)}) custom-call(bf16[256,128]{1,0:T(8,128)(2,1)S(1)} %reshape_reshape.3.values, f32[2,32,32,128]{3,2,1,0:T(8,128)S(1)} %get-tuple-element.21.table, ...), custom_call_target="tpu_custom_call" | custom-call | tf_op jit(solution)/shard_map/z_inputs/pallas_call | solution.py:467
  33.7 5.2 %z_lines.1 = f32[256,128]{1,0:T(8,128)S(1)} custom-call(f32[2,32,32,128]{3,2,1,0:T(8,128)S(1)} %get-tuple-element.21.table, bf16[4,2,32,128]{3,2,1,0:T(8,128)(2,1)S(1)} %get-tuple-element.22.wo, f32[16,32,128]{2,1,0:T(8,128)S(1)} %get-tuple-element.26.gate_s, f32[2,16,40,128]{3,2,1,0:T(8,128)S(1)} %get-tuple-element.27.sel_s, ...), custom_call_target="tpu_custom_call" | custom-call | tf_op jit(solution)/shard_map/z_lines/pallas_call | solution.py:486
  38.9 3.0 %all-to-all-done.1 = bf16[128,2,128]{2,1,0:T(2,128)(2,1)S(1)} async-done(((bf16[128,2,128]{2,1,0:T(2,128)(2,1)}), bf16[128,2,128]{2,1,0:T(2,128)(2,1)S(1)}, u32[]{:S(2)}, u32[]{:S(2)}) %all-to-all-start.1) | async-done | bytes 65568 | tf_op jit(solution)/shard_map/all_to_all | solution.py:515
  42.0 0.7 %fusion = bf16[1,2,16384]{2,1,0:T(2,128)(2,1)} fusion(f32[128,2,128]{2,1,0:T(2,128)S(1)} %bitcast.14, bf16[128,2,128]{2,1,0:T(2,128)(2,1)S(1)} %all-to-all-done.1), kind=kLoop, calls=%fused_computation.1 | loop fusion | flops 98304 | bytes 262144 | tf_op jit(solution)/shard_map/reshape | solution.py:518
Async XLA Ops:
  0.0 21.3 %all-to-all-start = ((bf16[128,2,128]{2,1,0:T(2,128)(2,1)}), bf16[128,2,128]{2,1,0:T(2,128)(2,1)S(1)}, u32[]{:S(2)}, u32[]{:S(2)}) async-start(bf16[128,2,128]{2,1,0:T(2,128)(2,1)} %bitcast.16), calls=%async_computation | async-start | bytes 131072 | tf_op jit(solution)/shard_map/all_to_all | solution.py:500
  28.0 4.2 %copy-start = (bf16[1,2,16384]{2,1,0:T(2,128)(2,1)S(1)}, bf16[1,2,16384]{2,1,0:T(2,128)(2,1)}, u32[]{:S(2)}) copy-start(bf16[1,2,16384]{2,1,0:T(2,128)(2,1)} %param.11) | copy-start | bytes 196612
  28.0 14.0 %all-to-all-start.1 = ((bf16[128,2,128]{2,1,0:T(2,128)(2,1)}), bf16[128,2,128]{2,1,0:T(2,128)(2,1)S(1)}, u32[]{:S(2)}, u32[]{:S(2)}) async-start(bf16[128,2,128]{2,1,0:T(2,128)(2,1)} %bitcast.8), calls=%async_computation.1 | async-start | bytes 131072 | tf_op jit(solution)/shard_map/all_to_all | solution.py:515

commit v4 on v3

--- a/solution.py
+++ b/solution.py
@@ -19,6 +19,8 @@
 STEPS = 16
 LINES = 32
 A0, CW0, DW0, CB0, DB0, SK0, ROWS = 0, 16, 20, 24, 25, 26, 32
+XW = 3
+SEL = 48
 LN2 = math.log(2.0)
 LOG2E = 1.0 / LN2
 F32 = jnp.float32
@@ -45,13 +47,15 @@
 
 def prepare_kernel(*refs):
     given, (vec, rate_far, w_step, w_in, w_out, gain2, swap), (table, lhsq, xp, wo) = refs[:10], refs[10:17], refs[17:21]
-    here, sem = refs[21:31], refs[31]
-    copies = [pltpu.make_async_copy(a, b, sem.at[i]) for i, (a, b) in enumerate(zip(given, here))]
+    here, sem = refs[21:30], refs[30]
+    names = [i for i in range(10) if i != XW]
+    copies = [pltpu.make_async_copy(given[i], here[at], sem.at[at]) for at, i in enumerate(names)]
     for copy in copies:
         copy.start()
     for copy in copies:
         copy.wait()
-    in_w, conv_w, conv_b, x_w, dt_w, dt_b, rate, skip, out_w, gain = here
+    in_w, conv_w, conv_b, dt_w, dt_b, rate, skip, out_w, gain = here
+    x_w = given[XW]
     row, column = iota((R + 2 * N, E), 0), iota((R + 2 * N, E), 1)
     pick = (row == column % (2 * N) + R).astype(F32)
     for d in range(2, 6):
@@ -89,7 +93,7 @@
     gain2[...] = jnp.concatenate([gain[...], gain[...]], axis=1)
     mask = ((iota((EQ, E), 1) % EQ) == iota((EQ, E), 0)).astype(BF16)
     same = (iota((2 * E, E), 0) % E // EQ == iota((2 * E, E), 1) // EQ).astype(BF16)
-    row, column = iota((40, 36), 0), iota((40, 36), 1)
+    row, column = iota((SEL, 36), 0), iota((SEL, 36), 1)
     pick = (column == jnp.where(row < 2 * N, row + R, row - 2 * N)) & (row < 2 * N + R)
     pick = pick.astype(BF16)
     for d in range(2):
@@ -141,7 +145,7 @@
         half = half + vec[CW + k : CW + k + 1, :] * taps[k]
     act = (half + half * jnp.tanh(half)).astype(BF16)
     both = jnp.dot(jnp.concatenate([act, act], axis=1), w_step, preferred_element_type=F32)
-    return act.astype(F32), softplus2(both[:, :E] + vec[DB : DB + 1, :]), both[:, E:]
+    return act, softplus2(both[:, :E] + vec[DB : DB + 1, :]), both[:, E:]
 
 
 def tree_sum(terms):
@@ -150,7 +154,7 @@
     return terms[0]
 
 
-def plane_kernel(values, vec, rate_far, w_step, w_in, w_out, gain2, swap, out, lines_s, normed_s, step_s, fresh_s, sel_s, step_t, fresh_t, sel_t, y_s, direct_s):
+def plane_kernel(values, vec, rate_far, w_step, w_in, w_out, gain2, swap, out, lines_s, normed_s, step_s, act_s, sel_s, step_t, fresh_t, sel_t, y_s, direct_s):
     normed = enter(values[...].astype(F32), gain2[...])
     normed_s[...] = normed
     both = jnp.dot(normed, w_in[:, : 2 * E], preferred_element_type=F32).astype(BF16)
@@ -174,18 +178,18 @@
                 firsts = [32 * (begin + (k if d == 0 else 6 - k)) for k in range(K)]
                 taps = [lines_s[axis, first : first + 128, :] for first in firsts]
                 act, step, sel = step_inputs(taps, vec[index], w_step[index])
-                direct_s[axis, d, begin * 32 : begin * 32 + 128, :] = vec[index, SK : SK + 1, :] * act
-                fresh = step * act
+                direct_s[axis, d, begin * 32 : begin * 32 + 128, :] = vec[index, SK : SK + 1, :] * act.astype(F32)
                 rows = slice(axis * 64 + d * 32, axis * 64 + d * 32 + 32)
                 for i in range(4):
                     t = i if d == 0 else 3 - i
                     lanes = slice(i * 32, i * 32 + 32)
                     step_s[4 * part + i, rows, :] = step[t * 32 : (t + 1) * 32]
-                    fresh_s[4 * part + i, rows, :] = fresh[t * 32 : (t + 1) * 32]
+                    act_s[4 * part + i, rows, :] = act[t * 32 : (t + 1) * 32]
                     sel_s[part, rows, lanes] = sel[t * 32 : (t + 1) * 32, lanes]
         for s in range(4 * part, 4 * part + 4):
-            step_t[s] = step_s[s].T
-            fresh_t[s] = fresh_s[s].T
+            step = step_s[s].T
+            step_t[s] = step
+            fresh_t[s] = step * act_s[s].T.astype(F32)
         sel_t[part * 128 : part * 128 + 128, :] = sel_s[part].T
 
     def group(g, carry):
@@ -424,18 +428,18 @@
         jax.ShapeDtypeStruct((256, 256), BF16),
         jax.ShapeDtypeStruct((2, ROWS, EQ, E), F32),
         jax.ShapeDtypeStruct((2 * EQ, Q * C), BF16),
-        jax.ShapeDtypeStruct((2, 40, E), BF16),
+        jax.ShapeDtypeStruct((2, SEL, E), BF16),
         jax.ShapeDtypeStruct((Q, 2, EQ, 2 * C), BF16),
     ]
     ready = pl.pallas_call(
         prepare_kernel,
         out_shape=shapes,
-        in_specs=[pl.BlockSpec(memory_space=pl.ANY)] * 10,
+        in_specs=[pl.BlockSpec(memory_space=pltpu.VMEM if i == XW else pl.ANY) for i in range(10)],
         out_specs=vmem(11),
-        scratch_shapes=[pltpu.VMEM(w.shape, w.dtype) for w in weights] + [pltpu.SemaphoreType.DMA((10,))],
+        scratch_shapes=[pltpu.VMEM(w.shape, w.dtype) for i, w in enumerate(weights) if i != XW] + [pltpu.SemaphoreType.DMA((9,))],
         compiler_params=PARAMS,
         name="prepare",
-    )(*[pltpu.with_memory_space_constraint(w, pltpu.HBM) for w in weights])
+    )(*[w if i == XW else pltpu.with_memory_space_constraint(w, pltpu.HBM) for i, w in enumerate(weights)])
     return ready[:7], (*ready[7:], ready[5])
 
 
@@ -449,7 +453,7 @@
             pltpu.VMEM((2, 704, E), F32),
             pltpu.VMEM((256, E), BF16),
             pltpu.VMEM((16, E, E), F32),
-            pltpu.VMEM((16, E, E), F32),
+            pltpu.VMEM((16, E, E), BF16),
             pltpu.VMEM((4, E, E), F32),
             pltpu.VMEM((16, E, E), F32),
             pltpu.VMEM((16, E, E), F32),
@@ -468,7 +472,7 @@
         line_inputs_kernel,
         out_shape=[
             jax.ShapeDtypeStruct((STEPS, EQ, E), F32),
-            jax.ShapeDtypeStruct((2, STEPS, 40, E), F32),
+            jax.ShapeDtypeStruct((2, STEPS, SEL, E), F32),
             jax.ShapeDtypeStruct((2, STEPS, EQ, E), F32),
             jax.ShapeDtypeStruct((2, STEPS, EQ, E), F32),
             jax.ShapeDtypeStruct((STEPS, EQ, E), F32),

time: 42.9 us -> 43 us (level)
  no operation moved by 1% of the time
where the time goes in v4:
time: 43 us; the launch traced here: 42.7 us
  starting transfers between devices  15.6 us (36%)
  Pallas kernels  15.4 us (36%)
  waiting for transfers between devices  10.8 us (25%)
  other arithmetic  0.7 us (2%)
    all_to_all x1, starting transfers between devices, local(): lax.all_to_all(sent, ('row', 'col'), split_axis=0, concat_axis=0, tiled=T...  11.5 us
    all_to_all x1, waiting for transfers between devices, local(): lax.all_to_all(sent, ('row', 'col'), split_axis=0, concat_axis=0, tiled=T...  7.84 us
    pallas_call x1, Pallas kernels, planes(): pl.pallas_call(plane_kernel, out_shape=jax.ShapeDtypeStruct((256, 2 * C),...  6.71 us
    pallas_call x1, Pallas kernels, z_lines(): pl.pallas_call(line_scan_kernel, out_shape=jax.ShapeDtypeStruct((256, 2 *...  5.21 us
    all_to_all x1, starting transfers between devices, local(): lax.all_to_all(far.reshape(128, 2, 2 * C), ('row', 'col'), split_axis=0,...  4.15 us
    all_to_all x1, waiting for transfers between devices, local(): lax.all_to_all(far.reshape(128, 2, 2 * C), ('row', 'col'), split_axis=0,...  2.97 us
    pallas_call x1, Pallas kernels, prepare(): pl.pallas_call(prepare_kernel, out_shape=shapes, in_specs=[pl.BlockSpec(m...  1.95 us
    pallas_call x1, Pallas kernels, z_inputs(): pl.pallas_call(line_inputs_kernel, out_shape=[jax.ShapeDtypeStruct((STEPS...  1.56 us
  transfers between devices with their start and end apart: 2, of which 2 were waited for; matrix products, arithmetic and copies ran while one was open for 0% of the time, Pallas kernels for 20%

profile of v4, /device:TPU:1, one launch (start us, length us, event | category | flops | bytes accessed | tf_op | source)
XLA Modules:
  0.0 42.7 jit_solution(18135659106976917618)
XLA Ops:
  0.0 0.0 copy-start
  0.0 11.5 %all-to-all-start = ((bf16[128,2,128]{2,1,0:T(2,128)(2,1)}), bf16[128,2,128]{2,1,0:T(2,128)(2,1)S(1)}, u32[]{:S(2)}, u32[]{:S(2)}) async-start(bf16[128,2,128]{2,1,0:T(2,128)(2,1)} %bitcast.17), calls=%async_computation | async-start | bytes 131072 | tf_op jit(solution)/shard_map/all_to_all | solution.py:504
  11.5 0.0 copy-done
  11.5 2.0 %prepare.1 = (f32[6,8,128]{2,1,0:T(8,128)S(1)}, f32[16,128,128]{2,1,0:T(8,128)S(1)}, bf16[6,256,256]{2,1,0:T(8,128)(2,1)S(1)}, bf16[128,512]{1,0:T(8,128)(2,1)S(...) custom-call(bf16[64,256]{1,0:T(8,128)(2,1)} %refs_0_.1, ...), custom_call_target="tpu_custom_call" | custom-call | tf_op jit(solution)/shard_map/prepare/pallas_call | solution.py:434
  13.5 7.8 %all-to-all-done = bf16[128,2,128]{2,1,0:T(2,128)(2,1)S(1)} async-done(((bf16[128,2,128]{2,1,0:T(2,128)(2,1)}), bf16[128,2,128]{2,1,0:T(2,128)(2,1)S(1)}, u32[]{:S(2)}, u32[]{:S(2)}) %all-to-all-start) | async-done | bytes 65568 | tf_op jit(solution)/shard_map/all_to_all | solution.py:504
  21.3 6.7 %planes.1 = bf16[256,128]{1,0:T(8,128)(2,1)} custom-call(bf16[256,128]{1,0:T(8,128)(2,1)S(1)} %bitcast.15, f32[6,8,128]{2,1,0:T(8,128)S(1)} %get-tuple-element.31.vec, f32[16,128,128]{2,1,0:T(8,128)S(1)} %get-tuple-element.32.rate_far, bf16[6,256,256]{2,1,0:T(8,128)(2,1)S(1)} %get-tuple-element.33.w_step, bf16[128,512]{1,0:T(8,128)(2,1)S(1)} %get-tuple-element.34.w_in, ...), custom_call_target="tpu_custom_call" | custom-call | tf_op jit(solution)/shard_map/planes/pallas_call | solution.py:447
  28.0 0.0 copy-start.1
  28.0 4.2 %all-to-all-start.1 = ((bf16[128,2,128]{2,1,0:T(2,128)(2,1)}), bf16[128,2,128]{2,1,0:T(2,128)(2,1)S(1)}, u32[]{:S(2)}, u32[]{:S(2)}) async-start(bf16[128,2,128]{2,1,0:T(2,128)(2,1)} %bitcast.8), calls=%async_computation.1 | async-start | bytes 131072 | tf_op jit(solution)/shard_map/all_to_all | solution.py:519
  32.2 0.0 copy-done.1
  32.2 0.1 reshape_reshape.3.values
  32.3 1.6 %z_inputs.1 = (f32[16,32,128]{2,1,0:T(8,128)S(1)}, f32[2,16,48,128]{3,2,1,0:T(8,128)S(1)}, f32[2,16,32,128]{3,2,1,0:T(8,128)S(1)}, f32[2,16,32,128]{3,2,1,0:T(8,128)S(1)}, f32[16,32,128]{2,1,0:T(8,128)S(1)}) custom-call(bf16[256,128]{1,0:T(8,128)(2,1)S(1)} %reshape_reshape.3.values, f32[2,32,32,128]{3,2,1,0:T(8,128)S(1)} %get-tuple-element.21.table, ...), custom_call_target="tpu_custom_call" | custom-call | tf_op jit(solution)/shard_map/z_inputs/pallas_call | solution.py:471
  33.8 5.2 %z_lines.1 = f32[256,128]{1,0:T(8,128)S(1)} custom-call(f32[2,32,32,128]{3,2,1,0:T(8,128)S(1)} %get-tuple-element.21.table, bf16[4,2,32,128]{3,2,1,0:T(8,128)(2,1)S(1)} %get-tuple-element.22.wo, f32[16,32,128]{2,1,0:T(8,128)S(1)} %get-tuple-element.26.gate_s, f32[2,16,48,128]{3,2,1,0:T(8,128)S(1)} %get-tuple-element.27.sel_s, ...), custom_call_target="tpu_custom_call" | custom-call | tf_op jit(solution)/shard_map/z_lines/pallas_call | solution.py:490
  39.0 3.0 %all-to-all-done.1 = bf16[128,2,128]{2,1,0:T(2,128)(2,1)S(1)} async-done(((bf16[128,2,128]{2,1,0:T(2,128)(2,1)}), bf16[128,2,128]{2,1,0:T(2,128)(2,1)S(1)}, u32[]{:S(2)}, u32[]{:S(2)}) %all-to-all-start.1) | async-done | bytes 65568 | tf_op jit(solution)/shard_map/all_to_all | solution.py:519
  42.0 0.7 %fusion = bf16[1,2,16384]{2,1,0:T(2,128)(2,1)} fusion(f32[128,2,128]{2,1,0:T(2,128)S(1)} %bitcast.14, bf16[128,2,128]{2,1,0:T(2,128)(2,1)S(1)} %all-to-all-done.1), kind=kLoop, calls=%fused_computation.1 | loop fusion | flops 98304 | bytes 262144 | tf_op jit(solution)/shard_map/reshape | solution.py:522
Async XLA Ops:
  0.0 11.5 %copy-start = (bf16[6,128,36]{1,2,0:T(8,128)(2,1)S(1)}, bf16[6,128,36]{1,2,0:T(8,128)(2,1)}, u32[]{:S(2)}) copy-start(bf16[6,128,36]{1,2,0:T(8,128)(2,1)} %param.16) | copy-start | bytes 165892
  0.0 21.3 %all-to-all-start = ((bf16[128,2,128]{2,1,0:T(2,128)(2,1)}), bf16[128,2,128]{2,1,0:T(2,128)(2,1)S(1)}, u32[]{:S(2)}, u32[]{:S(2)}) async-start(bf16[128,2,128]{2,1,0:T(2,128)(2,1)} %bitcast.17), calls=%async_computation | async-start | bytes 131072 | tf_op jit(solution)/shard_map/all_to_all | solution.py:504
  28.0 4.2 %copy-start.1 = (bf16[1,2,16384]{2,1,0:T(2,128)(2,1)S(1)}, bf16[1,2,16384]{2,1,0:T(2,128)(2,1)}, u32[]{:S(2)}) copy-start(bf16[1,2,16384]{2,1,0:T(2,128)(2,1)} %param.11) | copy-start | bytes 196612
  28.0 14.0 %all-to-all-start.1 = ((bf16[128,2,128]{2,1,0:T(2,128)(2,1)}), bf16[128,2,128]{2,1,0:T(2,128)(2,1)S(1)}, u32[]{:S(2)}, u32[]{:S(2)}) async-start(bf16[128,2,128]{2,1,0:T(2,128)(2,1)} %bitcast.8), calls=%async_computation.1 | async-start | bytes 131072 | tf_op jit(solution)/shard_map/all_to_all | solution.py:519

commit v5 on v4

--- a/solution.py
+++ b/solution.py
@@ -170,6 +170,7 @@
             lines_s[1, first : first + 16, :] = inner[h][i * 16 : (i + 1) * 16]
             lines_s[0, first : first + 16, :] = swapped[i * 16 : (i + 1) * 16, h * E : (h + 1) * E]
 
+    eye = (iota((E, E), 0) == iota((E, E), 1)).astype(BF16)
     for part in range(4):
         for axis in range(2):
             for d in range(2):
@@ -189,11 +190,12 @@
         for s in range(4 * part, 4 * part + 4):
             step = step_s[s].T
             step_t[s] = step
-            fresh_t[s] = step * act_s[s].T.astype(F32)
+            fresh_t[s] = step * lax.dot_general(eye, act_s[s], NT, preferred_element_type=F32)
         sel_t[part * 128 : part * 128 + 128, :] = sel_s[part].T
 
     def group(g, carry):
-        rows = [pl.ds(pl.multiple_of(g * 16 + 8 * i, 8), 8) for i in range(2)]
+        first = g * 16 if isinstance(g, int) else pl.multiple_of(g * 16, 16)
+        rows = [pl.ds(first + 8 * i, 8) for i in range(2)]
         results = []
         for i in range(2):
             rates = [rate_far[n, rows[i], :] for n in range(N)]
@@ -215,12 +217,14 @@
                 state = following
                 result.append(total[0] + total[1])
             results.append(result)
-        here = pl.ds(pl.multiple_of(g * 16, 16), 16)
+        here = pl.ds(first, 16)
         for s in range(16):
             y_s[s, here, :] = jnp.concatenate([results[0][s], results[1][s]], axis=0).astype(BF16)
         return carry
 
-    lax.fori_loop(0, 8, group, 0)
+    group(0, 0)
+    lax.fori_loop(1, 7, group, 0)
+    group(7, 0)
     gates = silu(jnp.dot(normed_s[...], w_in[:, 2 * E :], preferred_element_type=F32))
     turned = [y_s[s].T.astype(F32) for s in range(16)]
     sums = []

time: 43 us -> 42.9 us (level)
  no operation moved by 1% of the time
where the time goes in v5:
time: 42.9 us; the launch traced here: 42.6 us
  starting transfers between devices  15.7 us (37%)
  Pallas kernels  15.3 us (36%)
  waiting for transfers between devices  10.8 us (25%)
  other arithmetic  0.7 us (2%)
    all_to_all x1, starting transfers between devices, local(): lax.all_to_all(sent, ('row', 'col'), split_axis=0, concat_axis=0, tiled=T...  11.5 us
    all_to_all x1, waiting for transfers between devices, local(): lax.all_to_all(sent, ('row', 'col'), split_axis=0, concat_axis=0, tiled=T...  7.84 us
    pallas_call x1, Pallas kernels, planes(): pl.pallas_call(plane_kernel, out_shape=jax.ShapeDtypeStruct((256, 2 * C),...  6.61 us
    pallas_call x1, Pallas kernels, z_lines(): pl.pallas_call(line_scan_kernel, out_shape=jax.ShapeDtypeStruct((256, 2 *...  5.21 us
    all_to_all x1, starting transfers between devices, local(): lax.all_to_all(far.reshape(128, 2, 2 * C), ('row', 'col'), split_axis=0,...  4.15 us
    all_to_all x1, waiting for transfers between devices, local(): lax.all_to_all(far.reshape(128, 2, 2 * C), ('row', 'col'), split_axis=0,...  2.97 us
    pallas_call x1, Pallas kernels, prepare(): pl.pallas_call(prepare_kernel, out_shape=shapes, in_specs=[pl.BlockSpec(m...  1.95 us
    pallas_call x1, Pallas kernels, z_inputs(): pl.pallas_call(line_inputs_kernel, out_shape=[jax.ShapeDtypeStruct((STEPS...  1.56 us
  transfers between devices with their start and end apart: 2, of which 2 were waited for; matrix products, arithmetic and copies ran while one was open for 0% of the time, Pallas kernels for 20%

profile of v5, /device:TPU:1, one launch (start us, length us, event | category | flops | bytes accessed | tf_op | source)
XLA Modules:
  0.0 42.6 jit_solution(15850400048341591129)
XLA Ops:
  0.0 0.0 copy-start
  0.0 11.5 %all-to-all-start = ((bf16[128,2,128]{2,1,0:T(2,128)(2,1)}), bf16[128,2,128]{2,1,0:T(2,128)(2,1)S(1)}, u32[]{:S(2)}, u32[]{:S(2)}) async-start(bf16[128,2,128]{2,1,0:T(2,128)(2,1)} %bitcast.17), calls=%async_computation | async-start | bytes 131072 | tf_op jit(solution)/shard_map/all_to_all | solution.py:508
  11.5 0.0 copy-done
  11.5 2.0 %prepare.1 = (f32[6,8,128]{2,1,0:T(8,128)S(1)}, f32[16,128,128]{2,1,0:T(8,128)S(1)}, bf16[6,256,256]{2,1,0:T(8,128)(2,1)S(1)}, bf16[128,512]{1,0:T(8,128)(2,1)S(...) custom-call(bf16[64,256]{1,0:T(8,128)(2,1)} %refs_0_.1, ...), custom_call_target="tpu_custom_call" | custom-call | tf_op jit(solution)/shard_map/prepare/pallas_call | solution.py:438
  13.5 7.8 %all-to-all-done = bf16[128,2,128]{2,1,0:T(2,128)(2,1)S(1)} async-done(((bf16[128,2,128]{2,1,0:T(2,128)(2,1)}), bf16[128,2,128]{2,1,0:T(2,128)(2,1)S(1)}, u32[]{:S(2)}, u32[]{:S(2)}) %all-to-all-start) | async-done | bytes 65568 | tf_op jit(solution)/shard_map/all_to_all | solution.py:508
  21.3 6.6 %planes.1 = bf16[256,128]{1,0:T(8,128)(2,1)} custom-call(bf16[256,128]{1,0:T(8,128)(2,1)S(1)} %bitcast.15, f32[6,8,128]{2,1,0:T(8,128)S(1)} %get-tuple-element.31.vec, f32[16,128,128]{2,1,0:T(8,128)S(1)} %get-tuple-element.32.rate_far, bf16[6,256,256]{2,1,0:T(8,128)(2,1)S(1)} %get-tuple-element.33.w_step, bf16[128,512]{1,0:T(8,128)(2,1)S(1)} %get-tuple-element.34.w_in, ...), custom_call_target="tpu_custom_call" | custom-call | tf_op jit(solution)/shard_map/planes/pallas_call | solution.py:451
  27.9 0.0 copy-start.1
  27.9 4.2 %all-to-all-start.1 = ((bf16[128,2,128]{2,1,0:T(2,128)(2,1)}), bf16[128,2,128]{2,1,0:T(2,128)(2,1)S(1)}, u32[]{:S(2)}, u32[]{:S(2)}) async-start(bf16[128,2,128]{2,1,0:T(2,128)(2,1)} %bitcast.8), calls=%async_computation.1 | async-start | bytes 131072 | tf_op jit(solution)/shard_map/all_to_all | solution.py:523
  32.1 0.0 copy-done.1
  32.1 0.1 reshape_reshape.3.values
  32.2 1.6 %z_inputs.1 = (f32[16,32,128]{2,1,0:T(8,128)S(1)}, f32[2,16,48,128]{3,2,1,0:T(8,128)S(1)}, f32[2,16,32,128]{3,2,1,0:T(8,128)S(1)}, f32[2,16,32,128]{3,2,1,0:T(8,128)S(1)}, f32[16,32,128]{2,1,0:T(8,128)S(1)}) custom-call(bf16[256,128]{1,0:T(8,128)(2,1)S(1)} %reshape_reshape.3.values, f32[2,32,32,128]{3,2,1,0:T(8,128)S(1)} %get-tuple-element.21.table, ...), custom_call_target="tpu_custom_call" | custom-call | tf_op jit(solution)/shard_map/z_inputs/pallas_call | solution.py:475
  33.7 5.2 %z_lines.1 = f32[256,128]{1,0:T(8,128)S(1)} custom-call(f32[2,32,32,128]{3,2,1,0:T(8,128)S(1)} %get-tuple-element.21.table, bf16[4,2,32,128]{3,2,1,0:T(8,128)(2,1)S(1)} %get-tuple-element.22.wo, f32[16,32,128]{2,1,0:T(8,128)S(1)} %get-tuple-element.26.gate_s, f32[2,16,48,128]{3,2,1,0:T(8,128)S(1)} %get-tuple-element.27.sel_s, ...), custom_call_target="tpu_custom_call" | custom-call | tf_op jit(solution)/shard_map/z_lines/pallas_call | solution.py:494
  39.0 3.0 %all-to-all-done.1 = bf16[128,2,128]{2,1,0:T(2,128)(2,1)S(1)} async-done(((bf16[128,2,128]{2,1,0:T(2,128)(2,1)}), bf16[128,2,128]{2,1,0:T(2,128)(2,1)S(1)}, u32[]{:S(2)}, u32[]{:S(2)}) %all-to-all-start.1) | async-done | bytes 65568 | tf_op jit(solution)/shard_map/all_to_all | solution.py:523
  41.9 0.7 %fusion = bf16[1,2,16384]{2,1,0:T(2,128)(2,1)} fusion(f32[128,2,128]{2,1,0:T(2,128)S(1)} %bitcast.14, bf16[128,2,128]{2,1,0:T(2,128)(2,1)S(1)} %all-to-all-done.1), kind=kLoop, calls=%fused_computation.1 | loop fusion | flops 98304 | bytes 262144 | tf_op jit(solution)/shard_map/reshape | solution.py:526
Async XLA Ops:
  0.0 11.5 %copy-start = (bf16[6,128,36]{1,2,0:T(8,128)(2,1)S(1)}, bf16[6,128,36]{1,2,0:T(8,128)(2,1)}, u32[]{:S(2)}) copy-start(bf16[6,128,36]{1,2,0:T(8,128)(2,1)} %param.16) | copy-start | bytes 165892
  0.0 21.3 %all-to-all-start = ((bf16[128,2,128]{2,1,0:T(2,128)(2,1)}), bf16[128,2,128]{2,1,0:T(2,128)(2,1)S(1)}, u32[]{:S(2)}, u32[]{:S(2)}) async-start(bf16[128,2,128]{2,1,0:T(2,128)(2,1)} %bitcast.17), calls=%async_computation | async-start | bytes 131072 | tf_op jit(solution)/shard_map/all_to_all | solution.py:508
  27.9 4.2 %copy-start.1 = (bf16[1,2,16384]{2,1,0:T(2,128)(2,1)S(1)}, bf16[1,2,16384]{2,1,0:T(2,128)(2,1)}, u32[]{:S(2)}) copy-start(bf16[1,2,16384]{2,1,0:T(2,128)(2,1)} %param.11) | copy-start | bytes 196612
  27.9 14.0 %all-to-all-start.1 = ((bf16[128,2,128]{2,1,0:T(2,128)(2,1)}), bf16[128,2,128]{2,1,0:T(2,128)(2,1)S(1)}, u32[]{:S(2)}, u32[]{:S(2)}) async-start(bf16[128,2,128]{2,1,0:T(2,128)(2,1)} %bitcast.8), calls=%async_computation.1 | async-start | bytes 131072 | tf_op jit(solution)/shard_map/all_to_all | solution.py:523

commit v6 on v4

--- a/solution.py
+++ b/solution.py
@@ -518,8 +518,9 @@
     far = planes(arrived.reshape(256, 2 * C), ready)
     returned = lax.all_to_all(far.reshape(128, 2, 2 * C), ("row", "col"), split_axis=0, concat_axis=0, tiled=True)
     near = z_lines(given, z_ready)
-    mixed = (near.reshape(128, 2, 2 * C) + returned.astype(F32)).astype(BF16)
-    return mixed.transpose(1, 0, 2).reshape(1, 2, 128 * 2 * C)
+    mixed = (near + returned.reshape(256, 2 * C).astype(F32)).astype(BF16)
+    mixed = lax.optimization_barrier(mixed)
+    return mixed.reshape(128, 2, 2 * C).transpose(1, 0, 2).reshape(1, 2, 128 * 2 * C)
 
 
 def solution(mesh):

time: 43 us -> 43 us (level)
    reshape x1 -> x0, other arithmetic: 0.7 us -> none  [local(): return mixed.transpose(1, 0, 2).reshape(1, 2, 128 * 2 * C)]
    convert_element_type x0 -> x1, other arithmetic: none -> 0.65 us  [local(): mixed = (near + returned.reshape(256, 2 * C).astype(F32)).astype(BF16)]
where the time goes in v6:
time: 43 us; the launch traced here: 42.7 us
  starting transfers between devices  15.6 us (36%)
  Pallas kernels  15.4 us (36%)
  waiting for transfers between devices  10.8 us (25%)
  other arithmetic  0.65 us (2%)
    all_to_all x1, starting transfers between devices, local(): lax.all_to_all(sent, ('row', 'col'), split_axis=0, concat_axis=0, tiled=T...  11.5 us
    all_to_all x1, waiting for transfers between devices, local(): lax.all_to_all(sent, ('row', 'col'), split_axis=0, concat_axis=0, tiled=T...  7.84 us
    pallas_call x1, Pallas kernels, planes(): pl.pallas_call(plane_kernel, out_shape=jax.ShapeDtypeStruct((256, 2 * C),...  6.71 us
    pallas_call x1, Pallas kernels, z_lines(): pl.pallas_call(line_scan_kernel, out_shape=jax.ShapeDtypeStruct((256, 2 *...  5.21 us
    all_to_all x1, starting transfers between devices, local(): lax.all_to_all(far.reshape(128, 2, 2 * C), ('row', 'col'), split_axis=0,...  4.15 us
    all_to_all x1, waiting for transfers between devices, local(): lax.all_to_all(far.reshape(128, 2, 2 * C), ('row', 'col'), split_axis=0,...  2.97 us
    pallas_call x1, Pallas kernels, prepare(): pl.pallas_call(prepare_kernel, out_shape=shapes, in_specs=[pl.BlockSpec(m...  1.95 us
    pallas_call x1, Pallas kernels, z_inputs(): pl.pallas_call(line_inputs_kernel, out_shape=[jax.ShapeDtypeStruct((STEPS...  1.56 us
  transfers between devices with their start and end apart: 2, of which 2 were waited for; matrix products, arithmetic and copies ran while one was open for 0% of the time, Pallas kernels for 20%

profile of v6, /device:TPU:1, one launch (start us, length us, event | category | flops | bytes accessed | tf_op | source)
XLA Modules:
  0.0 42.7 jit_solution(14198014049382696175)
XLA Ops:
  0.0 0.0 copy-start
  0.0 11.5 %all-to-all-start = ((bf16[128,2,128]{2,1,0:T(2,128)(2,1)}), bf16[128,2,128]{2,1,0:T(2,128)(2,1)S(1)}, u32[]{:S(2)}, u32[]{:S(2)}) async-start(bf16[128,2,128]{2,1,0:T(2,128)(2,1)} %bitcast.18), calls=%async_computation | async-start | bytes 131072 | tf_op jit(solution)/shard_map/all_to_all | solution.py:504
  11.5 0.0 copy-done
  11.5 2.0 %prepare.1 = (f32[6,8,128]{2,1,0:T(8,128)S(1)}, f32[16,128,128]{2,1,0:T(8,128)S(1)}, bf16[6,256,256]{2,1,0:T(8,128)(2,1)S(1)}, bf16[128,512]{1,0:T(8,128)(2,1)S(...) custom-call(bf16[64,256]{1,0:T(8,128)(2,1)} %refs_0_.1, ...), custom_call_target="tpu_custom_call" | custom-call | tf_op jit(solution)/shard_map/prepare/pallas_call | solution.py:434
  13.5 7.8 %all-to-all-done = bf16[128,2,128]{2,1,0:T(2,128)(2,1)S(1)} async-done(((bf16[128,2,128]{2,1,0:T(2,128)(2,1)}), bf16[128,2,128]{2,1,0:T(2,128)(2,1)S(1)}, u32[]{:S(2)}, u32[]{:S(2)}) %all-to-all-start) | async-done | bytes 65568 | tf_op jit(solution)/shard_map/all_to_all | solution.py:504
  21.3 6.7 %planes.1 = bf16[256,128]{1,0:T(8,128)(2,1)} custom-call(bf16[256,128]{1,0:T(8,128)(2,1)S(1)} %bitcast.16, f32[6,8,128]{2,1,0:T(8,128)S(1)} %get-tuple-element.31.vec, f32[16,128,128]{2,1,0:T(8,128)S(1)} %get-tuple-element.32.rate_far, bf16[6,256,256]{2,1,0:T(8,128)(2,1)S(1)} %get-tuple-element.33.w_step, bf16[128,512]{1,0:T(8,128)(2,1)S(1)} %get-tuple-element.34.w_in, ...), custom_call_target="tpu_custom_call" | custom-call | tf_op jit(solution)/shard_map/planes/pallas_call | solution.py:447
  28.0 0.0 copy-start.1
  28.0 4.2 %all-to-all-start.1 = ((bf16[128,2,128]{2,1,0:T(2,128)(2,1)}), bf16[128,2,128]{2,1,0:T(2,128)(2,1)S(1)}, u32[]{:S(2)}, u32[]{:S(2)}) async-start(bf16[128,2,128]{2,1,0:T(2,128)(2,1)} %bitcast.7), calls=%async_computation.1 | async-start | bytes 131072 | tf_op jit(solution)/shard_map/all_to_all | solution.py:519
  32.2 0.0 copy-done.1
  32.2 0.1 reshape_reshape.3.values
  32.3 1.6 %z_inputs.1 = (f32[16,32,128]{2,1,0:T(8,128)S(1)}, f32[2,16,48,128]{3,2,1,0:T(8,128)S(1)}, f32[2,16,32,128]{3,2,1,0:T(8,128)S(1)}, f32[2,16,32,128]{3,2,1,0:T(8,128)S(1)}, f32[16,32,128]{2,1,0:T(8,128)S(1)}) custom-call(bf16[256,128]{1,0:T(8,128)(2,1)S(1)} %reshape_reshape.3.values, f32[2,32,32,128]{3,2,1,0:T(8,128)S(1)} %get-tuple-element.21.table, ...), custom_call_target="tpu_custom_call" | custom-call | tf_op jit(solution)/shard_map/z_inputs/pallas_call | solution.py:471
  33.8 5.2 %z_lines.1 = f32[256,128]{1,0:T(8,128)S(1)} custom-call(f32[2,32,32,128]{3,2,1,0:T(8,128)S(1)} %get-tuple-element.21.table, bf16[4,2,32,128]{3,2,1,0:T(8,128)(2,1)S(1)} %get-tuple-element.22.wo, f32[16,32,128]{2,1,0:T(8,128)S(1)} %get-tuple-element.26.gate_s, f32[2,16,48,128]{3,2,1,0:T(8,128)S(1)} %get-tuple-element.27.sel_s, ...), custom_call_target="tpu_custom_call" | custom-call | tf_op jit(solution)/shard_map/z_lines/pallas_call | solution.py:490
  39.0 3.0 %all-to-all-done.1 = bf16[128,2,128]{2,1,0:T(2,128)(2,1)S(1)} async-done(((bf16[128,2,128]{2,1,0:T(2,128)(2,1)}), bf16[128,2,128]{2,1,0:T(2,128)(2,1)S(1)}, u32[]{:S(2)}, u32[]{:S(2)}) %all-to-all-start.1) | async-done | bytes 65568 | tf_op jit(solution)/shard_map/all_to_all | solution.py:519
  42.0 0.7 %fusion = bf16[256,128]{1,0:T(8,128)(2,1)} fusion(f32[256,128]{1,0:T(8,128)S(1)} %z_lines.1, bf16[256,128]{1,0:T(8,128)(2,1)S(1)} %bitcast.19), kind=kLoop, calls=%fused_computation.1 | loop fusion | flops 98304 | bytes 262144 | tf_op jit(solution)/shard_map/convert_element_type | solution.py:521
Async XLA Ops:
  0.0 11.5 %copy-start = (bf16[6,128,36]{1,2,0:T(8,128)(2,1)S(1)}, bf16[6,128,36]{1,2,0:T(8,128)(2,1)}, u32[]{:S(2)}) copy-start(bf16[6,128,36]{1,2,0:T(8,128)(2,1)} %param.16) | copy-start | bytes 165892
  0.0 21.3 %all-to-all-start = ((bf16[128,2,128]{2,1,0:T(2,128)(2,1)}), bf16[128,2,128]{2,1,0:T(2,128)(2,1)S(1)}, u32[]{:S(2)}, u32[]{:S(2)}) async-start(bf16[128,2,128]{2,1,0:T(2,128)(2,1)} %bitcast.18), calls=%async_computation | async-start | bytes 131072 | tf_op jit(solution)/shard_map/all_to_all | solution.py:504
  28.0 4.2 %copy-start.1 = (bf16[1,2,16384]{2,1,0:T(2,128)(2,1)S(1)}, bf16[1,2,16384]{2,1,0:T(2,128)(2,1)}, u32[]{:S(2)}) copy-start(bf16[1,2,16384]{2,1,0:T(2,128)(2,1)} %param.11) | copy-start | bytes 196612
  28.0 14.0 %all-to-all-start.1 = ((bf16[128,2,128]{2,1,0:T(2,128)(2,1)}), bf16[128,2,128]{2,1,0:T(2,128)(2,1)S(1)}, u32[]{:S(2)}, u32[]{:S(2)}) async-start(bf16[128,2,128]{2,1,0:T(2,128)(2,1)} %bitcast.7), calls=%async_computation.1 | async-start | bytes 131072 | tf_op jit(solution)/shard_map/all_to_all | solution.py:519

commit v7 on v5

--- a/solution.py
+++ b/solution.py
@@ -172,7 +172,7 @@
 
     eye = (iota((E, E), 0) == iota((E, E), 1)).astype(BF16)
     for part in range(4):
-        for axis in range(2):
+        for axis in (1, 0):
             for d in range(2):
                 index = 2 + 2 * axis + d
                 begin = 4 * part if d == 0 else 12 - 4 * part

time: 42.9 us -> 43 us (level)
  no operation moved by 1% of the time
where the time goes in v7:
time: 43 us; the launch traced here: 42.7 us
  starting transfers between devices  15.7 us (37%)
  Pallas kernels  15.4 us (36%)
  waiting for transfers between devices  10.8 us (25%)
  other arithmetic  0.7 us (2%)
    all_to_all x1, starting transfers between devices, local(): lax.all_to_all(sent, ('row', 'col'), split_axis=0, concat_axis=0, tiled=T...  11.5 us
    all_to_all x1, waiting for transfers between devices, local(): lax.all_to_all(sent, ('row', 'col'), split_axis=0, concat_axis=0, tiled=T...  7.84 us
    pallas_call x1, Pallas kernels, planes(): pl.pallas_call(plane_kernel, out_shape=jax.ShapeDtypeStruct((256, 2 * C),...  6.68 us
    pallas_call x1, Pallas kernels, z_lines(): pl.pallas_call(line_scan_kernel, out_shape=jax.ShapeDtypeStruct((256, 2 *...  5.21 us
    all_to_all x1, starting transfers between devices, local(): lax.all_to_all(far.reshape(128, 2, 2 * C), ('row', 'col'), split_axis=0,...  4.15 us
    all_to_all x1, waiting for transfers between devices, local(): lax.all_to_all(far.reshape(128, 2, 2 * C), ('row', 'col'), split_axis=0,...  2.97 us
    pallas_call x1, Pallas kernels, prepare(): pl.pallas_call(prepare_kernel, out_shape=shapes, in_specs=[pl.BlockSpec(m...  1.95 us
    pallas_call x1, Pallas kernels, z_inputs(): pl.pallas_call(line_inputs_kernel, out_shape=[jax.ShapeDtypeStruct((STEPS...  1.56 us
  transfers between devices with their start and end apart: 2, of which 2 were waited for; matrix products, arithmetic and copies ran while one was open for 0% of the time, Pallas kernels for 20%

profile of v7, /device:TPU:1, one launch (start us, length us, event | category | flops | bytes accessed | tf_op | source)
XLA Modules:
  0.0 42.7 jit_solution(11265389483119481423)
XLA Ops:
  0.0 0.0 copy-start
  0.0 11.5 %all-to-all-start = ((bf16[128,2,128]{2,1,0:T(2,128)(2,1)}), bf16[128,2,128]{2,1,0:T(2,128)(2,1)S(1)}, u32[]{:S(2)}, u32[]{:S(2)}) async-start(bf16[128,2,128]{2,1,0:T(2,128)(2,1)} %bitcast.17), calls=%async_computation | async-start | bytes 131072 | tf_op jit(solution)/shard_map/all_to_all | solution.py:508
  11.5 0.0 copy-done
  11.5 2.0 %prepare.1 = (f32[6,8,128]{2,1,0:T(8,128)S(1)}, f32[16,128,128]{2,1,0:T(8,128)S(1)}, bf16[6,256,256]{2,1,0:T(8,128)(2,1)S(1)}, bf16[128,512]{1,0:T(8,128)(2,1)S(...) custom-call(bf16[64,256]{1,0:T(8,128)(2,1)} %refs_0_.1, ...), custom_call_target="tpu_custom_call" | custom-call | tf_op jit(solution)/shard_map/prepare/pallas_call | solution.py:438
  13.5 7.8 %all-to-all-done = bf16[128,2,128]{2,1,0:T(2,128)(2,1)S(1)} async-done(((bf16[128,2,128]{2,1,0:T(2,128)(2,1)}), bf16[128,2,128]{2,1,0:T(2,128)(2,1)S(1)}, u32[]{:S(2)}, u32[]{:S(2)}) %all-to-all-start) | async-done | bytes 65568 | tf_op jit(solution)/shard_map/all_to_all | solution.py:508
  21.3 6.7 %planes.1 = bf16[256,128]{1,0:T(8,128)(2,1)} custom-call(bf16[256,128]{1,0:T(8,128)(2,1)S(1)} %bitcast.15, f32[6,8,128]{2,1,0:T(8,128)S(1)} %get-tuple-element.31.vec, f32[16,128,128]{2,1,0:T(8,128)S(1)} %get-tuple-element.32.rate_far, bf16[6,256,256]{2,1,0:T(8,128)(2,1)S(1)} %get-tuple-element.33.w_step, bf16[128,512]{1,0:T(8,128)(2,1)S(1)} %get-tuple-element.34.w_in, ...), custom_call_target="tpu_custom_call" | custom-call | tf_op jit(solution)/shard_map/planes/pallas_call | solution.py:451
  28.0 0.0 copy-start.1
  28.0 4.2 %all-to-all-start.1 = ((bf16[128,2,128]{2,1,0:T(2,128)(2,1)}), bf16[128,2,128]{2,1,0:T(2,128)(2,1)S(1)}, u32[]{:S(2)}, u32[]{:S(2)}) async-start(bf16[128,2,128]{2,1,0:T(2,128)(2,1)} %bitcast.8), calls=%async_computation.1 | async-start | bytes 131072 | tf_op jit(solution)/shard_map/all_to_all | solution.py:523
  32.2 0.0 copy-done.1
  32.2 0.1 reshape_reshape.3.values
  32.2 1.6 %z_inputs.1 = (f32[16,32,128]{2,1,0:T(8,128)S(1)}, f32[2,16,48,128]{3,2,1,0:T(8,128)S(1)}, f32[2,16,32,128]{3,2,1,0:T(8,128)S(1)}, f32[2,16,32,128]{3,2,1,0:T(8,128)S(1)}, f32[16,32,128]{2,1,0:T(8,128)S(1)}) custom-call(bf16[256,128]{1,0:T(8,128)(2,1)S(1)} %reshape_reshape.3.values, f32[2,32,32,128]{3,2,1,0:T(8,128)S(1)} %get-tuple-element.21.table, ...), custom_call_target="tpu_custom_call" | custom-call | tf_op jit(solution)/shard_map/z_inputs/pallas_call | solution.py:475
  33.8 5.2 %z_lines.1 = f32[256,128]{1,0:T(8,128)S(1)} custom-call(f32[2,32,32,128]{3,2,1,0:T(8,128)S(1)} %get-tuple-element.21.table, bf16[4,2,32,128]{3,2,1,0:T(8,128)(2,1)S(1)} %get-tuple-element.22.wo, f32[16,32,128]{2,1,0:T(8,128)S(1)} %get-tuple-element.26.gate_s, f32[2,16,48,128]{3,2,1,0:T(8,128)S(1)} %get-tuple-element.27.sel_s, ...), custom_call_target="tpu_custom_call" | custom-call | tf_op jit(solution)/shard_map/z_lines/pallas_call | solution.py:494
  39.0 3.0 %all-to-all-done.1 = bf16[128,2,128]{2,1,0:T(2,128)(2,1)S(1)} async-done(((bf16[128,2,128]{2,1,0:T(2,128)(2,1)}), bf16[128,2,128]{2,1,0:T(2,128)(2,1)S(1)}, u32[]{:S(2)}, u32[]{:S(2)}) %all-to-all-start.1) | async-done | bytes 65568 | tf_op jit(solution)/shard_map/all_to_all | solution.py:523
  42.0 0.7 %fusion = bf16[1,2,16384]{2,1,0:T(2,128)(2,1)} fusion(f32[128,2,128]{2,1,0:T(2,128)S(1)} %bitcast.14, bf16[128,2,128]{2,1,0:T(2,128)(2,1)S(1)} %all-to-all-done.1), kind=kLoop, calls=%fused_computation.1 | loop fusion | flops 98304 | bytes 262144 | tf_op jit(solution)/shard_map/reshape | solution.py:526
Async XLA Ops:
  0.0 11.5 %copy-start = (bf16[6,128,36]{1,2,0:T(8,128)(2,1)S(1)}, bf16[6,128,36]{1,2,0:T(8,128)(2,1)}, u32[]{:S(2)}) copy-start(bf16[6,128,36]{1,2,0:T(8,128)(2,1)} %param.16) | copy-start | bytes 165892
  0.0 21.3 %all-to-all-start = ((bf16[128,2,128]{2,1,0:T(2,128)(2,1)}), bf16[128,2,128]{2,1,0:T(2,128)(2,1)S(1)}, u32[]{:S(2)}, u32[]{:S(2)}) async-start(bf16[128,2,128]{2,1,0:T(2,128)(2,1)} %bitcast.17), calls=%async_computation | async-start | bytes 131072 | tf_op jit(solution)/shard_map/all_to_all | solution.py:508
  28.0 4.2 %copy-start.1 = (bf16[1,2,16384]{2,1,0:T(2,128)(2,1)S(1)}, bf16[1,2,16384]{2,1,0:T(2,128)(2,1)}, u32[]{:S(2)}) copy-start(bf16[1,2,16384]{2,1,0:T(2,128)(2,1)} %param.11) | copy-start | bytes 196612
  28.0 14.0 %all-to-all-start.1 = ((bf16[128,2,128]{2,1,0:T(2,128)(2,1)}), bf16[128,2,128]{2,1,0:T(2,128)(2,1)S(1)}, u32[]{:S(2)}, u32[]{:S(2)}) async-start(bf16[128,2,128]{2,1,0:T(2,128)(2,1)} %bitcast.8), calls=%async_computation.1 | async-start | bytes 131072 | tf_op jit(solution)/shard_map/all_to_all | solution.py:523
